TPU v7x, 512 devices: a whole 4x8x8 slice. The times are simulated.
512 devices in a mesh: gx: 8 (over z), gy: 4 (over x), gz: 16 (over y, core).
Axes of the slice: x: 4, y: 8, z: 8, core: 2. Of those that a mesh axis runs over, the one named last changes fastest.
Arguments:
- body_forces: float32 [3, 64, 32, 2048], P(None, 'gx', 'gy', 'gz'), may hold values from -8 to 8, as said below
- material: int32 [64, 32, 2048], P('gx', 'gy', 'gz'), may hold values from 0 to 15
- fixed_mask: int32 [64, 32, 2048], P('gx', 'gy', 'gz'), may hold values 0 or 1
- moduli: float32 [2, 16], replicated, may hold values from 0.05 to 1
Outputs:
- displacement: float32 [3, 64, 32, 2048], P(None, 'gx', 'gy', 'gz')
- residual: float32 [3, 64, 32, 2048], P(None, 'gx', 'gy', 'gz')
Inputs may be any that keep to these rules, and one draw needn't show every extreme that they name: `body_forces`: forces on the voxels, of order one.
All inputs are finite; a program needn't handle non-finite values. No bound on the sum of `fixed_mask` on one device may be relied on, other than what follows from the above.
Results may differ from a plain program's by a relative error of at most 0.0001.
Values sent between devices are 32-bit elements; how exact they have to be, the bound alone decides.
No kernel may reach another device: no remote copies, remote signals or barrier semaphores. Data moves between devices by JAX's collectives and lax.ppermute only.
A program may use at most 128 MiB of HBM per device.

v0:
```python
import jax
import jax.numpy as jnp
from jax import lax
from jax.sharding import PartitionSpec as P

SMOOTH = 4
AGX = 1
AGY = 1
AGZ = 16
CLASSES = 16


CHEB_CENTER = 1.125
CHEB_HALF = 0.875


def with_halo(shard, sides, width):
    for axis, dim in sides:
        count, length = (lax.axis_size(axis), shard.shape[dim])
        up = [(i, (i + 1) % count) for i in range(count - 1)]
        down = [(j, i) for i, j in up]
        last = lax.slice_in_dim(shard, length - width, length, axis=dim)
        first = lax.slice_in_dim(shard, 0, width, axis=dim)
        before = lax.ppermute(last, axis, up)
        after = lax.ppermute(first, axis, down)
        shard = jnp.concatenate([before, shard, after], axis=dim)
    return shard


def coarsen(values, factor_x, factor_y, factor_z, method):
    leading = values.shape[:-3]
    size_x, size_y, size_z = values.shape[-3:]
    blocks = values.reshape(
        leading
        + (size_x // factor_x, factor_x, size_y // factor_y, factor_y, size_z // factor_z, factor_z)
    )
    offset = len(leading)
    summed_axes = (offset + 1, offset + 3, offset + 5)
    if method == "mean":
        return jnp.mean(blocks, axis=summed_axes)
    if method == "most":
        return jnp.max(blocks, axis=summed_axes)
    return jnp.sum(blocks, axis=summed_axes)


def prolong(values, factor_x, factor_y, factor_z):
    return jnp.repeat(
        jnp.repeat(jnp.repeat(values, factor_x, axis=-3), factor_y, axis=-2), factor_z, axis=-1
    )


def pad_zero(values):
    return jnp.pad(values, ((0, 0), (1, 1), (1, 1), (1, 1)))


def field_halo(values):
    return with_halo(values, (("gx", 1), ("gy", 2), ("gz", 3)), 1)


def material_halo(values):
    return with_halo(values, (("gx", 1), ("gy", 2), ("gz", 3)), 1)


def arrange(gathered, block_shape):
    count_x = lax.axis_size("gx")
    count_y = lax.axis_size("gy")
    count_z = lax.axis_size("gz")
    depth_dim, size_x, size_y, size_z = block_shape
    arranged = gathered.reshape((count_x, count_y, count_z, depth_dim, size_x, size_y, size_z))
    arranged = jnp.transpose(arranged, (3, 0, 4, 1, 5, 2, 6))
    return arranged.reshape((depth_dim, count_x * size_x, count_y * size_y, count_z * size_z))


def collect_material(block_values):
    gathered = lax.all_gather(block_values[None], ("gx", "gy", "gz"), axis=0, tiled=True)
    return arrange(gathered, block_values.shape)


def collect_residual(block_values):
    gathered = lax.all_gather(block_values[None], ("gx", "gy", "gz"), axis=0, tiled=True)
    return arrange(gathered, block_values.shape)


def own_block(whole_grid, block_shape):
    zero_start = jnp.zeros((), jnp.int32)
    start_x = lax.axis_index("gx") * block_shape[1]
    start_y = lax.axis_index("gy") * block_shape[2]
    start_z = lax.axis_index("gz") * block_shape[3]
    return lax.dynamic_slice(whole_grid, (zero_start, start_x, start_y, start_z), block_shape)


def prepare(material_now, active, scales, pad_material):
    padded = pad_material(material_now)
    face_vals = (
        0.5 * scales[0] * (padded[:, :-1, 1:-1, 1:-1] + padded[:, 1:, 1:-1, 1:-1]),
        0.5 * scales[1] * (padded[:, 1:-1, :-1, 1:-1] + padded[:, 1:-1, 1:, 1:-1]),
        0.5 * scales[2] * (padded[:, 1:-1, 1:-1, :-1] + padded[:, 1:-1, 1:-1, 1:]),
    )
    coefficients = []
    diagonals = []
    for component in range(3):
        stiff_row = []
        summed = jnp.zeros(active.shape, jnp.float32)
        for direction in range(3):
            facing = face_vals[direction]
            if component == direction:
                stiffness = facing[0] + (facing[1] + facing[0])
            else:
                stiffness = facing[0]
            length = active.shape[direction]
            summed = (
                summed
                + lax.slice_in_dim(stiffness, 0, length, axis=direction)
                + lax.slice_in_dim(stiffness, 1, length + 1, axis=direction)
            )
            stiff_row.append(stiffness)
        coefficients.append(stiff_row)
        diagonals.append(summed)
    diagonal = jnp.stack(diagonals)
    inverse = 1.0 / (active * diagonal + (1.0 - active))
    return (coefficients, diagonal, active, inverse)


def operate(values, level_data, pad_field):
    coefficients, diagonal, active, inverse = level_data
    masked = active * values
    padded = pad_field(masked)
    results = []
    for component in range(3):
        component_field = padded[component]
        summed = diagonal[component] * masked[component]
        neighbours = (
            (component_field[:-2, 1:-1, 1:-1], component_field[2:, 1:-1, 1:-1]),
            (component_field[1:-1, :-2, 1:-1], component_field[1:-1, 2:, 1:-1]),
            (component_field[1:-1, 1:-1, :-2], component_field[1:-1, 1:-1, 2:]),
        )
        for direction in range(3):
            stiffness = coefficients[component][direction]
            length = masked.shape[1 + direction]
            lower_faces = lax.slice_in_dim(stiffness, 0, length, axis=direction)
            upper_faces = lax.slice_in_dim(stiffness, 1, length + 1, axis=direction)
            summed = (
                summed
                - lower_faces * neighbours[direction][0]
                - upper_faces * neighbours[direction][1]
            )
        results.append(summed)
    return active * jnp.stack(results) + (1.0 - active) * values


def smooth(solution, residual, level_data, pad_field):
    inverse = level_data[3]
    center_ratio = CHEB_CENTER / CHEB_HALF
    rho_now = 1.0 / center_ratio
    update = inverse * residual / CHEB_CENTER
    for sweep_index in range(3):
        solution = solution + update
        residual = residual - operate(update, level_data, pad_field)
        if sweep_index < 2:
            rho_next = 1.0 / (2.0 * center_ratio - rho_now)
            update = rho_next * rho_now * update + 2.0 * rho_next / CHEB_HALF * inverse * residual
            rho_now = rho_next
    return (solution, residual)


def assemble(level_data):
    coefficients, diagonal, active, inverse = level_data
    grid_shape = active.shape
    cell_count = grid_shape[0] * grid_shape[1] * grid_shape[2]
    strides = (grid_shape[1] * grid_shape[2], grid_shape[2], 1)
    positions = jnp.arange(cell_count, dtype=jnp.int32)
    flat_active = active.reshape(cell_count)
    matrices = []
    for component in range(3):
        matrix = jnp.diag(diagonal[component].reshape(cell_count))
        for direction in range(3):
            length = grid_shape[direction]
            upper_faces = lax.slice_in_dim(
                coefficients[component][direction], 1, length + 1, axis=direction
            )
            inside = lax.broadcasted_iota(jnp.int32, grid_shape, direction) < length - 1
            link_values = jnp.where(inside, upper_faces, jnp.zeros_like(upper_faces)).reshape(
                cell_count
            )
            pattern = (positions[None, :] == positions[:, None] + strides[direction]).astype(
                jnp.float32
            )
            coupling = link_values[:, None] * pattern
            matrix = matrix - coupling - coupling.T
        matrix = flat_active[:, None] * matrix * flat_active[None, :] + jnp.diag(1.0 - flat_active)
        matrices.append(matrix)
    return jnp.stack(matrices)


def coarse_solve(factors, right_side):
    flat_side = right_side.reshape(3, -1)
    solved = jax.vmap(lambda factor, column: jax.scipy.linalg.cho_solve((factor, True), column))(
        factors, flat_side
    )
    return solved.reshape(right_side.shape)


def coarse_correction(factors, whole_residual):
    coarse_side = coarsen(whole_residual, AGX, AGY, AGZ, "sum")
    return prolong(coarse_solve(factors, coarse_side), AGX, AGY, AGZ)


def coarse_scales():
    extent_x = float(2 ** (SMOOTH - 1) * AGX)
    extent_y = float(2 ** (SMOOTH - 1) * AGY)
    extent_z = float(2 ** (SMOOTH - 1) * AGZ)
    return (
        extent_y * extent_z / extent_x,
        extent_x * extent_z / extent_y,
        extent_x * extent_y / extent_z,
    )


def descend(depth_now, right_side, level_list, finish):
    level_data = level_list[depth_now]
    solution, residual = smooth(jnp.zeros_like(right_side), right_side, level_data, field_halo)
    if depth_now + 1 < len(level_list):
        lower_solution = descend(
            depth_now + 1, coarsen(residual, 2, 2, 2, "sum"), level_list, finish
        )[0]
        correction = prolong(lower_solution, 2, 2, 2)
    else:
        correction = finish(residual)
    solution = solution + correction
    residual = residual - operate(correction, level_data, field_halo)
    return smooth(solution, residual, level_data, field_halo)


def body(body_forces, material, fixed_mask, moduli):
    class_ids = jnp.arange(CLASSES, dtype=jnp.int32)
    class_hits = material[None] == class_ids[:, None, None, None]
    shear_modulus = jnp.sum(jnp.where(class_hits, moduli[0][:, None, None, None], 0.0), axis=0)
    lame_modulus = jnp.sum(jnp.where(class_hits, moduli[1][:, None, None, None], 0.0), axis=0)
    materials = [jnp.stack([shear_modulus, lame_modulus])]
    actives = [(1 - fixed_mask).astype(jnp.float32)]
    for level_index in range(1, SMOOTH):
        materials.append(coarsen(materials[-1], 2, 2, 2, "mean"))
        actives.append(coarsen(actives[-1], 2, 2, 2, "most"))
    spread = SMOOTH
    base_level = min(spread, SMOOTH - 1)
    whole_stack = collect_material(
        jnp.concatenate([materials[base_level], actives[base_level][None]], axis=0)
    )
    whole_material = whole_stack[:2]
    whole_active = whole_stack[2]
    level_index = 3
    level_scale = float(2**level_index)
    coarse_level = prepare(
        coarsen(whole_material, AGX, AGY, AGZ, "mean"),
        coarsen(whole_active, AGX, AGY, AGZ, "most"),
        coarse_scales(),
        pad_zero,
    )
    factors = jnp.linalg.cholesky(assemble(coarse_level))

    def finish(residual):
        whole_rest = collect_residual(residual)
        return own_block(coarse_correction(factors, whole_rest), residual.shape)

    level_list = []
    for level_index in range(spread):
        level_scale = float(2**level_index)
        level_list.append(
            prepare(
                materials[level_index],
                actives[level_index],
                (level_scale, level_scale, level_scale),
                material_halo,
            )
        )
    displacement, residual = descend(0, body_forces, level_list, finish)
    return (displacement, residual)


def solution(mesh):
    return jax.shard_map(
        body,
        mesh=mesh,
        in_specs=(P(None, "gx", "gy", "gz"), P("gx", "gy", "gz"), P("gx", "gy", "gz"), P()),
        out_specs=(P(None, "gx", "gy", "gz"), P(None, "gx", "gy", "gz")),
        check_vma=False,
    )
```

profile of v0, /device:TPU:224, one launch (start us, length us, event | category | flops | bytes accessed | tf_op | source)
XLA Modules:
  0.0 1479.2 jit_solution(10990427274874191157)
XLA Ops:
  12.7 5.5 collective-permute-start.66
  20.7 5.1 collective-permute-start.18
  35.1 73.4 %all-gather = f32[1536,1,1,16]{3,2,1,0:T(1,128)S(1)} all-gather(f32[3,1,1,16]{3,2,1,0:T(1,128)S(1)} %copy.3022), channel_id=2, replica_groups=mesh['gx'=8,'gy'=4,'gz'=16] {'gx','gy','gz'}, dimensions={0}, use_global_device_ids=true | all-gather | bytes 98496 | tf_op jit(solution)/shard_map/all_gather | solution.py:75
  131.7 35.2 %custom-call.38 = f32[3,128,128]{2,1,0:T(8,128)S(1)} custom-call(f32[3,128,128]{2,1,0:T(8,128)S(1)} %cholesky.274), custom_call_target="Cholesky" | custom-call | tf_op jit(solution)/shard_map/jit(cholesky)/cholesky | solution.py:259
  168.0 30.9 %custom-call.39 = f32[3,1,128,128]{2,3,1,0:T(8,128)} custom-call(f32[3,1,128,128]{3,2,1,0:T(8,128)} %select_bitcast_fusion.2), custom_call_target="InvertDiagBlocksLowerTriangular" | custom-call | tf_op jit(solution)/shard_map/jit(cholesky)/cholesky | solution.py:259
  204.0 37.0 %custom-call.40 = f32[3,128,128]{2,1,0:T(8,128)} custom-call(f32[3,128,128]{2,1,0:T(8,128)} %cholesky.278), custom_call_target="Cholesky" | custom-call | tf_op jit(solution)/shard_map/jit(cholesky)/cholesky | solution.py:259
  242.6 30.9 %custom-call.41 = f32[3,1,128,128]{2,3,1,0:T(8,128)} custom-call(f32[3,1,128,128]{3,2,1,0:T(8,128)} %get-tuple-element.121), custom_call_target="InvertDiagBlocksLowerTriangular" | custom-call | tf_op jit(solution)/shard_map/jit(cholesky)/cholesky | solution.py:259
  278.4 36.6 %custom-call.42 = f32[3,128,128]{2,1,0:T(8,128)} custom-call(f32[3,128,128]{2,1,0:T(8,128)} %cholesky.283), custom_call_target="Cholesky" | custom-call | tf_op jit(solution)/shard_map/jit(cholesky)/cholesky | solution.py:259
  316.7 31.1 %custom-call.43 = f32[3,1,128,128]{2,3,1,0:T(8,128)} custom-call(f32[3,1,128,128]{3,2,1,0:T(8,128)} %get-tuple-element.119), custom_call_target="InvertDiagBlocksLowerTriangular" | custom-call | tf_op jit(solution)/shard_map/jit(cholesky)/cholesky | solution.py:259
  351.6 36.6 %custom-call.44 = f32[3,128,128]{2,1,0:T(8,128)} custom-call(f32[3,128,128]{2,1,0:T(8,128)} %convolution_subtract_fusion.2), custom_call_target="Cholesky" | custom-call | tf_op jit(solution)/shard_map/jit(cholesky)/cholesky | solution.py:259
  416.0 5.1 collective-permute-start.68
  432.9 4.6 collective-permute-start.2
  441.1 4.9 collective-permute-start.5
  450.7 5.1 collective-permute-start.6
  473.2 5.0 collective-permute-done.10
  482.0 5.1 collective-permute-start.12
  489.1 4.9 collective-permute-start.23
  508.8 5.0 collective-permute-done.16
  517.4 5.1 collective-permute-start.24
  538.3 5.0 collective-permute-done.28
  545.0 7.6 reshape.3725
  558.0 5.4 collective-permute-start.30
  566.1 4.5 collective-permute-start.32
  583.4 5.4 collective-permute-start.36
  594.5 4.8 collective-permute-start.38
  606.3 4.9 collective-permute-done.40
  613.8 5.1 collective-permute-start.48
  621.6 4.5 collective-permute-start.50
  671.2 5.4 collective-permute-start.54
  699.6 5.1 collective-permute-start.60
  731.6 5.1 collective-permute-start.72
  764.2 5.4 collective-permute-start.78
  773.7 5.4 collective-permute-start.80
  780.3 13.6 while.1
  799.7 119.4 %custom-call.45 = f32[3,4,128,128]{2,3,1,0:T(8,128)} custom-call(f32[3,4,128,128]{3,2,1,0:T(8,128)} %bitcast.1520), custom_call_target="InvertDiagBlocksLowerTriangular" | custom-call | tf_op jit(solution)/shard_map/vmap(jit(_cho_solve))/triangular_solve | solution.py:197
  925.7 5.5 collective-permute-start.84
  935.3 5.1 collective-permute-start.86
  947.1 4.6 collective-permute-done.88
  958.4 5.2 collective-permute-start.90
  967.7 5.4 collective-permute-start.92
  988.2 82.1 %all_gather.7 = f32[512,3,1,1,16]{4,3,2,1,0:T(1,128)} all-gather(f32[1,3,1,1,16]{4,3,2,1,0:T(1,128)S(1)} %copy.3060), channel_id=1, replica_groups=mesh['gx'=8,'gy'=4,'gz'=16] {'gx','gy','gz'}, dimensions={0}, use_global_device_ids=true | all-gather | bytes 98496 | tf_op jit(solution)/shard_map/all_gather | solution.py:80
  1070.3 4.6 reduce_sum.130
  1150.3 4.8 collective-permute-start.104
  1177.7 4.8 collective-permute-start.110
  1198.3 5.4 collective-permute-start.114
  1206.4 4.8 collective-permute-start.116
  1226.1 5.4 collective-permute-start.120
  1234.1 4.8 collective-permute-start.122
  1253.8 5.4 collective-permute-start.126
  1261.8 4.8 collective-permute-start.128
  1282.1 5.4 collective-permute-start.132
  1290.2 4.8 collective-permute-start.134
  1308.0 5.4 collective-permute-start.138
  1316.0 4.8 collective-permute-start.140
  1333.6 5.4 collective-permute-start.144
  1341.6 4.8 collective-permute-start.146
  1360.6 5.4 collective-permute-start.150
  1382.6 5.0 collective-permute-done.154
  1391.4 5.4 collective-permute-start.156
  1413.1 5.0 collective-permute-done.160
  1421.6 5.4 collective-permute-start.162
  1443.4 5.0 collective-permute-done.166
  1452.0 5.4 collective-permute-start.168
  1471.8 5.0 collective-permute-done.172
  (1119 shorter events, 686.9 us)
Async XLA Ops:
  10.8 384.2 %collective-permute-start.67 = (f32[2,1,1,16]{3,0,2,1:T(2,128)S(1)}, f32[2,1,1,16]{3,0,2,1:T(2,128)}, u32[]{:S(2)}, u32[]{:S(2)}) collective-permute-start(f32[2,1,1,16]{3,0,2,1:T(2,128)S(1)} %multiply_bitcast_fusion), channel_id=1, source_target_pairs={{64,0},{128,64},{192,128},{256,192},{320,256},{384,320},{448,384},... | collective-permute-start | bytes 392 | tf_op jit(solution)/shard_map/ppermute | solution.py:25
  12.7 385.4 %collective-permute-start.66 = (f32[2,1,1,16]{3,0,2,1:T(2,128)S(1)}, f32[2,1,1,16]{3,0,2,1:T(2,128)}, u32[]{:S(2)}, u32[]{:S(2)}) collective-permute-start(f32[2,1,1,16]{3,0,2,1:T(2,128)S(1)} %multiply_bitcast_fusion), channel_id=1, source_target_pairs={{0,64},{64,128},{128,192},{192,256},{256,320},{320,384},{384,448},... | collective-permute-start | bytes 392 | tf_op jit(solution)/shard_map/ppermute | solution.py:24
  18.8 397.2 %collective-permute-start.19 = (f32[2,1,4,64]{3,2,1,0:T(4,128)}, f32[2,1,4,64]{3,2,1,0:T(4,128)}, u32[]{:S(2)}, u32[]{:S(2)}) collective-permute-start(f32[2,1,4,64]{3,2,1,0:T(4,128)} %get-tuple-element.297), channel_id=1, source_target_pairs={{64,0},{128,64},{192,128},{256,192},{320,256},{384,320},{448,384},... | collective-permute-start | bytes 6152 | tf_op jit(solution)/shard_map/ppermute | solution.py:25
  20.7 400.4 %collective-permute-start.18 = (f32[2,1,4,64]{3,2,1,0:T(4,128)}, f32[2,1,4,64]{3,2,1,0:T(4,128)}, u32[]{:S(2)}, u32[]{:S(2)}) collective-permute-start(f32[2,1,4,64]{3,2,1,0:T(4,128)} %get-tuple-element.296), channel_id=1, source_target_pairs={{0,64},{64,128},{128,192},{192,256},{256,320},{320,384},{384,448},... | collective-permute-start | bytes 6152 | tf_op jit(solution)/shard_map/ppermute | solution.py:24
  26.5 405.0 %collective-permute-start.1 = (f32[2,1,8,128]{3,2,1,0:T(8,128)}, f32[2,1,8,128]{3,2,1,0:T(8,128)S(1)}, u32[]{:S(2)}, u32[]{:S(2)}) collective-permute-start(f32[2,1,8,128]{3,2,1,0:T(8,128)} %get-tuple-element.191), channel_id=1, source_target_pairs={{64,0},{128,64},{192,128},{256,192},{320,256},{384,320},{448,384},... | collective-permute-start | bytes 24584 | tf_op jit(solution)/shard_map/ppermute | solution.py:25
  394.9 9.7 collective-permute-start.43
  405.9 8.7 collective-permute-start.44
  410.6 21.0 %collective-permute-start = (f32[2,1,8,128]{3,2,1,0:T(8,128)S(1)}, f32[2,1,8,128]{3,2,1,0:T(8,128)S(1)}, u32[]{:S(2)}, u32[]{:S(2)}) collective-permute-start(f32[2,1,8,128]{3,2,1,0:T(8,128)S(1)} %copy-done.115), channel_id=1, source_target_pairs={{0,64},{64,128},{128,192},{192,256},{256,320},{320,384},{384,448},... | collective-permute-start | bytes 24584 | tf_op jit(solution)/shard_map/ppermute | solution.py:24
  414.7 262.0 %collective-permute-start.69 = (f32[2,3,1,16]{3,0,2,1:T(2,128)}, f32[2,3,1,16]{3,0,2,1:T(2,128)}, u32[]{:S(2)}, u32[]{:S(2)}) collective-permute-start(f32[2,3,1,16]{3,0,2,1:T(2,128)} %pad_maximum_fusion.148), channel_id=1, source_target_pairs={{16,0},{32,16},{48,32},{17,1},{33,17},{49,33},{18,2},{34,18},{50,3... | collective-permute-start | bytes 1160 | tf_op jit(solution)/shard_map/ppermute | solution.py:25
  416.0 260.6 %collective-permute-start.68 = (f32[2,3,1,16]{3,0,2,1:T(2,128)}, f32[2,3,1,16]{3,0,2,1:T(2,128)}, u32[]{:S(2)}, u32[]{:S(2)}) collective-permute-start(f32[2,3,1,16]{3,0,2,1:T(2,128)} %pad_maximum_fusion.148), channel_id=1, source_target_pairs={{0,16},{16,32},{32,48},{1,17},{17,33},{33,49},{2,18},{18,34},{34,5... | collective-permute-start | bytes 1160 | tf_op jit(solution)/shard_map/ppermute | solution.py:24
  439.2 7.2 collective-permute-start.4
  441.1 7.1 collective-permute-start.5
  448.7 7.2 collective-permute-start.7
  470.0 8.3 collective-permute-start.10
  479.9 9.2 collective-permute-start.13
  482.0 11.9 collective-permute-start.12
  487.1 10.5 collective-permute-start.22
  489.1 8.6 collective-permute-start.23
  505.5 8.3 collective-permute-start.16
  515.4 7.1 collective-permute-start.25
  535.0 8.3 collective-permute-start.28
  556.1 7.4 collective-permute-start.31
  574.0 6.9 collective-permute-start.34
  581.5 9.3 collective-permute-start.37
  583.4 9.8 collective-permute-start.36
  590.8 8.6 collective-permute-start.46
  611.8 7.1 collective-permute-start.49
  620.3 13.8 collective-permute-start.51
  621.6 12.5 collective-permute-start.50
  634.9 15.8 %collective-permute-start.53 = (f32[3,6,6,1]{3,2,1,0:T(8,128)}, f32[3,6,6,1]{3,2,1,0:T(8,128)}, u32[]{:S(2)}, u32[]{:S(2)}) collective-permute-start(f32[3,6,6,1]{3,2,1,0:T(8,128)} %get-tuple-element.176), channel_id=1, source_target_pairs={{1,0},{2,1},{3,2},{4,3},{5,4},{6,5},{7,6},{8,7},{9,8},{10,9},{11,1... | collective-permute-start | bytes 1304 | tf_op jit(solution)/shard_map/ppermute | solution.py:25
  636.8 13.9 collective-permute-start.52
  669.3 8.1 collective-permute-start.55
  697.7 11.4 collective-permute-start.61
  699.6 9.5 collective-permute-start.60
  704.8 17.1 %collective-permute-start.71 = (f32[2,3,3,1]{3,0,2,1:T(2,128)S(1)}, f32[2,3,3,1]{3,0,2,1:T(2,128)S(1)}, u32[]{:S(2)}, u32[]{:S(2)}) collective-permute-start(f32[2,3,3,1]{3,0,2,1:T(2,128)S(1)} %get-tuple-element.314), channel_id=1, source_target_pairs={{1,0},{2,1},{3,2},{4,3},{5,4},{6,5},{7,6},{8,7},{9,8},{10,9},{11,1... | collective-permute-start | bytes 224 | tf_op jit(solution)/shard_map/ppermute | solution.py:25
  706.7 15.2 %collective-permute-start.70 = (f32[2,3,3,1]{3,0,2,1:T(2,128)S(1)}, f32[2,3,3,1]{3,0,2,1:T(2,128)S(1)}, u32[]{:S(2)}, u32[]{:S(2)}) collective-permute-start(f32[2,3,3,1]{3,0,2,1:T(2,128)S(1)} %get-tuple-element.313), channel_id=1, source_target_pairs={{0,1},{1,2},{2,3},{3,4},{4,5},{5,6},{6,7},{7,8},{8,9},{9,10},{10,1... | collective-permute-start | bytes 224 | tf_op jit(solution)/shard_map/ppermute | solution.py:24
  729.7 7.1 collective-permute-start.73
  762.3 7.3 collective-permute-start.79
  764.2 6.9 collective-permute-start.78
  772.4 21.5 %collective-permute-start.81 = (f32[3,3,1,16]{3,2,1,0:T(1,128)}, f32[3,3,1,16]{3,2,1,0:T(1,128)}, u32[]{:S(2)}, u32[]{:S(2)}) collective-permute-start(f32[3,3,1,16]{3,2,1,0:T(1,128)} %pad_maximum_fusion.130), channel_id=1, source_target_pairs={{16,0},{32,16},{48,32},{17,1},{33,17},{49,33},{18,2},{34,18},{50,3... | collective-permute-start | bytes 1736 | tf_op jit(solution)/shard_map/ppermute | solution.py:25
  773.7 20.2 %collective-permute-start.80 = (f32[3,3,1,16]{3,2,1,0:T(1,128)}, f32[3,3,1,16]{3,2,1,0:T(1,128)}, u32[]{:S(2)}, u32[]{:S(2)}) collective-permute-start(f32[3,3,1,16]{3,2,1,0:T(1,128)} %pad_maximum_fusion.130), channel_id=1, source_target_pairs={{0,16},{16,32},{32,48},{1,17},{17,33},{33,49},{2,18},{18,34},{34,5... | collective-permute-start | bytes 1736 | tf_op jit(solution)/shard_map/ppermute | solution.py:24
  795.3 123.7 %collective-permute-start.83 = (f32[3,3,3,1]{3,2,1,0:T(4,128)}, f32[3,3,3,1]{3,2,1,0:T(4,128)}, u32[]{:S(2)}, u32[]{:S(2)}) collective-permute-start(f32[3,3,3,1]{3,2,1,0:T(4,128)} %get-tuple-element.293), channel_id=1, source_target_pairs={{1,0},{2,1},{3,2},{4,3},{5,4},{6,5},{7,6},{8,7},{9,8},{10,9},{11,1... | collective-permute-start | bytes 332 | tf_op jit(solution)/shard_map/ppermute | solution.py:25
  797.3 121.8 %collective-permute-start.82 = (f32[3,3,3,1]{3,2,1,0:T(4,128)}, f32[3,3,3,1]{3,2,1,0:T(4,128)}, u32[]{:S(2)}, u32[]{:S(2)}) collective-permute-start(f32[3,3,3,1]{3,2,1,0:T(4,128)} %get-tuple-element.292), channel_id=1, source_target_pairs={{0,1},{1,2},{2,3},{3,4},{4,5},{5,6},{6,7},{7,8},{8,9},{9,10},{10,1... | collective-permute-start | bytes 332 | tf_op jit(solution)/shard_map/ppermute | solution.py:24
  923.8 7.4 collective-permute-start.85
  925.7 7.0 collective-permute-start.84
  956.5 7.1 collective-permute-start.91
  1112.9 7.1 collective-permute-start.97
  1140.3 7.2 collective-permute-start.103
  1168.1 7.1 collective-permute-start.109
  1196.4 7.3 collective-permute-start.115
  1224.2 7.3 collective-permute-start.121
  1251.9 7.3 collective-permute-start.127
  1280.2 7.3 collective-permute-start.133
  1306.0 7.3 collective-permute-start.139
  1331.7 7.3 collective-permute-start.145
  1350.0 6.9 collective-permute-start.148
  1358.6 7.3 collective-permute-start.151
  1379.3 8.3 collective-permute-start.154
  1389.4 7.3 collective-permute-start.157
  1409.9 8.3 collective-permute-start.160
  1419.7 7.3 collective-permute-start.163
  1440.2 8.3 collective-permute-start.166
  1450.0 7.3 collective-permute-start.169
  1468.5 8.3 collective-permute-start.172
  (237 other events, 9846.2 us)
where the time goes:
time: 1490 us; the launch traced here: 1480 us
  starting transfers between devices  508 us (34%)
  other arithmetic  487 us (33%)
  waiting for transfers between devices  193 us (13%)
  blocking collectives  155 us (10%)
  local copies, waits for them, and re-layouts  104 us (7%)
  matrix products  25 us (2%)
    ppermute x87, starting transfers between devices, with_halo(): before = lax.ppermute(last, axis, up)  344 us
    another operation x18, other arithmetic, body(): factors = jnp.linalg.cholesky(assemble(coarse_level))  245 us
    ppermute x87, starting transfers between devices, with_halo(): after = lax.ppermute(first, axis, down)  164 us
    ppermute x87, waiting for transfers between devices, with_halo(): before = lax.ppermute(last, axis, up)  152 us
    another operation x15, other arithmetic, coarse_solve(): jax.scipy.linalg.cho_solve((factor, True), column)  132 us
    all_gather x1, blocking collectives, collect_residual(): lax.all_gather(block_values[None], ('gx', 'gy', 'gz'), axis=0, tiled=True)  82.1 us
    all_gather x1, blocking collectives, collect_material(): lax.all_gather(block_values[None], ('gx', 'gy', 'gz'), axis=0, tiled=True)  73.4 us
    ppermute x87, waiting for transfers between devices, with_halo(): after = lax.ppermute(first, axis, down)  40.9 us
  transfers between devices with their start and end apart: 174, of which 85 were waited for; matrix products, arithmetic and copies ran while one was open for 33% of the time, Pallas kernels for 0%

commit v1 on v0

v1 whole, which is shorter than its diff:
```python
import jax
import jax.numpy as jnp
from jax import lax
from jax.experimental import pallas as pl
from jax.experimental.pallas import tpu as pltpu
from jax.sharding import PartitionSpec as P

F32 = jnp.float32
CLASSES = 16
THETA = 1.125
HALF = 0.875
SIGMA = THETA / HALF
VMEM_LIMIT = 50 * 1024 * 1024


def cheb_factors():
    rho = 1.0 / SIGMA
    found = []
    for _ in range(2):
        rho_next = 1.0 / (2.0 * SIGMA - rho)
        found.append((rho_next * rho, 2.0 * rho_next / HALF))
        rho = rho_next
    return found


CHEB = cheb_factors()
START = (0.0, 1.0 / THETA)


def dot(a, b):
    return lax.dot_general(
        a, b, (((1,), (0,)), ((), ())), precision=lax.Precision.HIGHEST, preferred_element_type=F32
    )


def dot_nt(a, b):
    return lax.dot_general(
        a, b, (((1,), (1,)), ((), ())), precision=lax.Precision.HIGHEST, preferred_element_type=F32
    )


def iota(shape, dim):
    return lax.broadcasted_iota(jnp.int32, shape, dim)


def ones_where(cond):
    return jnp.where(cond, 1.0, 0.0).astype(F32)


def roll(v, shift, axis):
    size = v.shape[axis]
    return pltpu.roll(v, shift % size, axis)


def neighbours_y(v, rows_masked):
    down, up = roll(v, 1, 0), roll(v, -1, 0)
    if rows_masked:
        row = iota(v.shape, 0)
        down = jnp.where(row >= 1, down, 0.0)
        up = jnp.where(row <= v.shape[0] - 2, up, 0.0)
    return down, up


def plane_factors(mod, scale, faces, diag, inv, lo, hi, rows_masked):
    half = 0.5 * scale

    def body(i, carry):
        def fields(j):
            shear, lame = mod[0, j], mod[1, j]
            return half * shear, half * (shear + lame)

        p, g = fields(i)
        pm, gm = fields(i - 1)
        pp, gp = fields(i + 1)
        a, am = mod[2, i], mod[2, i - 1]
        pyd, pyu = neighbours_y(p, rows_masked)
        gyd, gyu = neighbours_y(g, rows_masked)
        ayd, _ = neighbours_y(a, rows_masked)
        pzd, pzu = roll(p, 1, 1), roll(p, -1, 1)
        gzd, gzu = roll(g, 1, 1), roll(g, -1, 1)
        azd = roll(a, 1, 1)
        base = (pm + pp) + (pyd + pyu) + (pzd + pzu) + 6.0 * p
        extra = (gm + gp, gyd + gyu, gzd + gzu)
        for c in range(3):
            d = a * (base + (extra[c] + 2.0 * g)) + (1.0 - a)
            diag[c, i] = d
            inv[c, i] = 1.0 / d
        for k, (pn, gn, an) in enumerate(((pm, gm, am), (pyd, gyd, ayd), (pzd, gzd, azd))):
            both = a * an
            face = p + pn
            faces[2 * k, i] = both * face
            faces[2 * k + 1, i] = both * (face + (g + gn))
        return carry

    lax.fori_loop(lo, hi, body, 0)


def plane_sweep(d, d_next, r_in, r_out, faces, diag, inv, lo, hi, pair, r_in_at=0, r_out_at=0):
    def body(i, carry):
        for c in range(3):
            fx = faces[1 if c == 0 else 0, i]
            fxu = faces[1 if c == 0 else 0, i + 1]
            fy = faces[3 if c == 1 else 2, i]
            fz = faces[5 if c == 2 else 4, i]
            dc = d[c, i]
            t = fx * d[c, i - 1] + fxu * d[c, i + 1]
            t = t + (fy * roll(dc, 1, 0) + roll(fy * dc, -1, 0))
            t = t + (fz * roll(dc, 1, 1) + roll(fz * dc, -1, 1))
            r = r_in[c, i - r_in_at] - (diag[c, i] * dc - t)
            if r_out is not None:
                r_out[c, i - r_out_at] = r
            if pair is not None:
                new = (pair[1] * inv[c, i]) * r
                if pair[0] != 0.0:
                    new = new + pair[0] * dc
                d_next[c, i] = new
        return carry

    lax.fori_loop(lo, hi, body, 0)


def kernel_a(moduli, ext, send, r_out, x_out, mod, faces, diag, inv, d_a, d_b, r):
    def look_up(i, carry):
        mat = ext[3, i]
        shear = jnp.zeros(mat.shape, F32)
        lame = jnp.zeros(mat.shape, F32)
        for k in range(CLASSES):
            hit = mat == float(k + 1)
            shear = jnp.where(hit, moduli[0, k], shear)
            lame = jnp.where(hit, moduli[1, k], lame)
        mod[0, i] = shear
        mod[1, i] = lame
        mod[2, i] = ext[4, i]
        return carry

    lax.fori_loop(0, 22, look_up, 0)
    plane_factors(mod, 1.0, faces, diag, inv, 1, 21, False)

    def start(i, carry):
        for c in range(3):
            d_a[c, i] = (START[1] * inv[c, i]) * ext[c, i]
        return carry

    lax.fori_loop(1, 21, start, 0)
    plane_sweep(d_a, d_b, ext, r, faces, diag, inv, 2, 20, CHEB[0])
    for c in range(3):
        x_out[c] = d_a[c, 7:15, 0:8, 0:128] + d_b[c, 7:15, 0:8, 0:128]
    plane_sweep(d_b, d_a, r, r, faces, diag, inv, 3, 19, CHEB[1])
    for c in range(3):
        x_out[c] = x_out[c] + d_a[c, 7:15, 0:8, 0:128]
    plane_sweep(d_a, None, r, r_out, faces, diag, inv, 4, 18, None, 0, 4)
    rows = []
    for c in range(3):
        for j in range(4):
            rows.append(r_out[c, 3 + 2 * j, 0:8] + r_out[c, 4 + 2 * j, 0:8])
    for k in range(3):
        for j in range(4):
            rows.append(mod[k, 7 + 2 * j, 0:8] + mod[k, 8 + 2 * j, 0:8])
    stacked = jnp.concatenate(rows, axis=0)
    pair_z = ones_where(iota((256, 128), 0) // 2 == iota((256, 128), 1))
    pair_y = ones_where(iota((96, 192), 1) // 2 == iota((96, 192), 0))
    low = dot(pair_y, dot(stacked, pair_z))
    row = iota((96, 128), 0)
    low = jnp.where(row < 48, low, jnp.where(row < 80, 0.125 * low, ones_where(low > 0.5)))
    send[...] = low


def flat_factors(mods, steps, scales, groups):
    shear, lame, a = mods
    total = 0.0
    faces = []
    for (axis, shift, below, above), scale, share in zip(steps, scales, groups):
        h = (0.5 * scale) * (shear + share * (shear + lame))
        dn, up = roll(h, shift, axis), roll(h, -shift, axis)
        an = roll(a, shift, axis)
        if below is not None:
            dn = jnp.where(below, dn, 0.0)
            up = jnp.where(above, up, 0.0)
            an = jnp.where(below, an, 0.0)
        total = total + (2.0 * h + (dn + up))
        faces.append((a * an) * (h + dn))
    diag = a * total + (1.0 - a)
    return faces, diag, 1.0 / diag


def flat_apply(v, factors, steps):
    faces, diag, inv = factors
    out = diag * v
    for face, (axis, shift, below, above) in zip(faces, steps):
        out = out - (face * roll(v, shift, axis) + roll(face * v, -shift, axis))
    return out


def flat_smooth(x, r, factors, steps, last):
    inv = factors[2]
    d = (START[1] * inv) * r
    for sweep in range(3):
        x = d if x is None else x + d
        if sweep == 2 and not last:
            return x, None
        r = r - flat_apply(d, factors, steps)
        if sweep < 2:
            c1, c2 = CHEB[sweep]
            d = c1 * d + (c2 * inv) * r
    return x, r


def level2_steps():
    lane = iota((64, 128), 1)
    return (
        (1, 8, lane >= 8, lane < 120),
        (1, 1, lane % 8 >= 1, lane % 8 <= 6),
        (0, 1, None, None),
    )


def level3_steps(rows):
    lane = iota((rows, 128), 1)
    row = iota((rows, 128), 0)
    return (
        (1, 4, lane % 32 >= 4, lane % 32 < 28),
        (1, 1, lane % 4 >= 1, lane % 4 <= 2),
        (0, 1, row >= 1, row <= rows - 2),
    )


def level3_groups(rows):
    group = iota((rows, 128), 1) // 32
    return tuple(ones_where(group == k) for k in range(3))


def to_level3(k):
    cell = iota((128, 128), 0)
    lane = iota((128, 128), 1)
    return ones_where(lane == 32 * k + (cell // 16) * 4 + (cell % 8) // 2)


def kernel_b(got, send, mod1, x1, r1, mod2, x2, r2, faces, diag, inv, d_a, d_b, b1):
    sub = iota((8, 128), 0) < 4
    zero = jnp.zeros((16, 128), F32)
    for k in range(3):
        mod1[k, 0] = zero
        mod1[k, 33] = zero
        d_a[k, 0] = zero
        d_a[k, 33] = zero
        d_b[k, 0] = zero
        d_b[k, 33] = zero
    for k in range(6):
        faces[k, 33] = zero

    def unpack(gx, carry):
        for f in range(6):
            for pair in range(2):
                at = f * 16 + pair * 8
                for half in range(2):
                    s0 = got[gx * 4 + 2 * half, at : at + 8]
                    s1 = got[gx * 4 + 2 * half + 1, at : at + 8]
                    even = jnp.where(sub, s0, roll(s1, 4, 0))
                    odd = jnp.where(sub, roll(s0, 4, 0), s1)
                    x = gx * 4 + 2 * pair + 1
                    rows = slice(8 * half, 8 * half + 8)
                    if f < 3:
                        b1[f, x, rows] = even
                        b1[f, x + 1, rows] = odd
                    else:
                        mod1[f - 3, x, rows] = even
                        mod1[f - 3, x + 1, rows] = odd
        return carry

    lax.fori_loop(0, 8, unpack, 0)
    plane_factors(mod1, 2.0, faces, diag, inv, 1, 33, True)

    def start(i, carry):
        for c in range(3):
            d_a[c, i] = (START[1] * inv[c, i]) * b1[c, i]
        return carry

    lax.fori_loop(1, 33, start, 0)
    plane_sweep(d_a, d_b, b1, r1, faces, diag, inv, 1, 33, CHEB[0])
    for c in range(3):
        x1[c] = d_a[c] + d_b[c]
    plane_sweep(d_b, d_a, r1, r1, faces, diag, inv, 1, 33, CHEB[1])
    for c in range(3):
        x1[c] = x1[c] + d_a[c]
    plane_sweep(d_a, None, r1, r1, faces, diag, inv, 1, 33, None)

    pair_y = ones_where(iota((128, 256), 1) // 2 == iota((128, 256), 0))
    pair_z = ones_where(iota((64, 128), 1) // 2 == iota((64, 128), 0))

    def restrict(ref, k):
        planes = [ref[k, 1 + 2 * j] + ref[k, 2 + 2 * j] for j in range(16)]
        return dot_nt(pair_z, dot(pair_y, jnp.concatenate(planes, axis=0)))

    shear = 0.125 * restrict(mod1, 0)
    lame = 0.125 * restrict(mod1, 1)
    active = ones_where(restrict(mod1, 2) > 0.5)
    mod2[0] = shear
    mod2[1] = lame
    mod2[2] = active
    steps = level2_steps()
    own_z = ones_where(iota((16, 64), 1) // 2 == iota((16, 64), 0))
    low = jnp.zeros((16, 128), F32)
    for c in range(3):
        shares = tuple(1.0 if c == k else 0.0 for k in range(3))
        factors = flat_factors((shear, lame, active), steps, (4.0, 4.0, 4.0), shares)
        x, r = flat_smooth(None, restrict(r1, c), factors, steps, True)
        x2[c] = x
        r2[c] = r
        low = low + dot(dot(own_z, r), to_level3(c))
    send[0] = low
    lane = iota((16, 128), 1)
    low = dot(dot(own_z, shear), to_level3(0)) + dot(dot(own_z, lame), to_level3(1))
    low = 0.125 * low
    low = low + ones_where(dot(dot(own_z, active), to_level3(2)) > 0.5)
    send[1] = low


def spread(v, group):
    lane = iota(v.shape, 1)
    v = jnp.where(lane // 32 == group, v, 0.0)
    back = roll(v, -32 * group, 1)
    return back + roll(back, 32, 1) + roll(back, 64, 1)


def coarse_solve(mods3, rest, mat):
    blocks = ones_where(iota((16, 256), 1) // 16 == iota((16, 256), 0))
    shear = 0.0625 * dot(blocks, mods3[0])
    lame = 0.0625 * dot(blocks, mods3[1])
    active = ones_where(dot(blocks, mods3[2]) > 0.5)
    side = dot(blocks, rest)
    steps = level3_steps(16)
    scales = (128.0, 128.0, 0.5)
    faces, diag, _ = flat_factors((shear, lame, active), steps, scales, level3_groups(16))
    columns = [diag, side]
    for face, (axis, shift, below, above) in zip(faces, steps):
        columns.append(face)
        columns.append(jnp.where(above, roll(face, -shift, axis), 0.0))
    stacked = jnp.concatenate(columns, axis=0).T
    row = iota((32, 128), 0)
    lane = iota((32, 128), 1)
    patterns = (
        ones_where(lane == row),
        ones_where(lane == 96),
        -ones_where((lane == row - 4) & (lane < 32)),
        -ones_where((lane == row + 4) & (lane < 32)),
        -ones_where((lane == row - 1) & (lane < 32)),
        -ones_where((lane == row + 1) & (lane < 32)),
        -ones_where(lane == row + 32),
        -ones_where(lane == row + 64),
    )
    for c in range(3):
        part = stacked[32 * c : 32 * c + 32]
        for k in range(16):
            m = 0.0
            for q in range(8):
                at = 16 * q + k
                m = m + part[:, at : at + 1] * patterns[q]
            mat[c, k] = m

    def eliminate(cells):
        a = jnp.stack([mat[c, k] for c, k in cells])
        rows = iota(a.shape, 1)
        for p in range(32):
            pivot = a[:, p : p + 1, :]
            pivot = pivot * (1.0 / a[:, p : p + 1, p : p + 1])
            a = jnp.where(rows == p, pivot, a - a[:, :, p : p + 1] * pivot)
        for n, (c, k) in enumerate(cells):
            mat[c, k] = a[n]

    lane_t = lane < 32
    lane_l = (lane >= 32) & (lane < 64)
    lane_r = (lane >= 64) & (lane < 96)
    lane_b = lane >= 96
    keep = lane_t | lane_b
    none = jnp.zeros((32, 128), F32)
    for h in (1, 2, 4, 8):
        eliminate([(c, k) for c in range(3) for k in range(h, 16, 2 * h)])
        for c in range(3):
            for k in range(0, 16, 2 * h):
                m = mat[c, k]
                left, right = none, none
                if k - h >= 0:
                    w = mat[c, k - h]
                    left = jnp.where(lane_t, roll(w, 64, 1), jnp.where(lane_l | lane_b, w, 0.0))
                if k + h < 16:
                    w = mat[c, k + h]
                    right = jnp.where(lane_t, roll(w, 96, 1), jnp.where(lane_r | lane_b, w, 0.0))
                change = dot(m, jnp.concatenate([none, left, right, none], axis=0))
                mat[c, k] = jnp.where(keep, m, 0.0) - change
    eliminate([(c, 0) for c in range(3)])
    picked = lane == 96
    first_row = ones_where(row == 0)
    pieces = []
    for c in range(3):
        found = {}
        last = jnp.where(picked, mat[c, 0], 0.0)
        found[0] = jnp.broadcast_to(jnp.sum(last, axis=1, keepdims=True), (32, 128))
        for h in (8, 4, 2, 1):
            for k in range(h, 16, 2 * h):
                after = -found[k + h] if k + h < 16 else none
                v = jnp.concatenate([none, -found[k - h], after, first_row], axis=0)
                found[k] = dot(mat[c, k], v)
        piece = none
        for k in range(16):
            piece = jnp.where(lane == k, found[k], piece)
        pieces.append(piece)
    pieces.append(none)
    whole = jnp.concatenate(pieces, axis=0)
    again = ones_where(iota((256, 128), 0) // 16 == iota((256, 128), 1))
    return dot_nt(again, whole)


def kernel_c(
    place, got, mod1, x1, r1, mod2, x2, r2, mod0, x0, r0, disp, resid,
    mat, e3, e1, faces1, diag1, inv1, d1a, d1b, r1w, faces, diag, inv, d_a, d_b, r_w,
):
    gx, gy, gz = place[0], place[1], place[2]
    b3 = jnp.concatenate([got[k, 0] for k in range(16)], axis=0)
    m3 = jnp.concatenate([got[k, 1] for k in range(16)], axis=0)
    mods3 = tuple(spread(m3, k) for k in range(3))
    steps = level3_steps(256)
    factors = flat_factors(mods3, steps, (8.0, 8.0, 8.0), level3_groups(256))
    x, r = flat_smooth(None, b3, factors, steps, True)
    corr = coarse_solve(mods3, r, mat)
    x = x + corr
    r = r - flat_apply(corr, factors, steps)
    x, _ = flat_smooth(x, r, factors, steps, False)
    e3[0:8] = jnp.zeros((8, 128), F32)
    e3[264:272] = jnp.zeros((8, 128), F32)
    e3[8:264] = x
    base = pl.multiple_of(gz * 16, 16)
    own = e3[pl.ds(base + 8, 24)]
    before = e3[pl.ds(base, 8)]
    slab = jnp.concatenate([own, before], axis=0)
    slab = dot(ones_where(iota((64, 32), 0) // 2 == iota((64, 32), 1)), slab)
    steps = level2_steps()
    mods = (mod2[0], mod2[1], mod2[2])
    for k in range(3):
        e1[k, 0] = jnp.zeros((16, 128), F32)
        e1[k, 33] = jnp.zeros((16, 128), F32)
        d1a[k, 0] = jnp.zeros((16, 128), F32)
        d1a[k, 33] = jnp.zeros((16, 128), F32)
        d1b[k, 0] = jnp.zeros((16, 128), F32)
        d1b[k, 33] = jnp.zeros((16, 128), F32)
    for k in range(6):
        faces1[k, 33] = jnp.zeros((16, 128), F32)
    up_xy = ones_where(
        ((iota((512, 128), 0) // 32) * 8 + (iota((512, 128), 0) % 16) // 2) == iota((512, 128), 1)
    )
    up_z = ones_where(iota((64, 128), 1) // 2 == iota((64, 128), 0))
    for c in range(3):
        shares = tuple(1.0 if c == k else 0.0 for k in range(3))
        factors = flat_factors(mods, steps, (4.0, 4.0, 4.0), shares)
        corr = dot_nt(slab, to_level3(c))
        x = x2[c] + corr
        r = r2[c] - flat_apply(corr, factors, steps)
        x, _ = flat_smooth(x, r, factors, steps, False)
        lifted = dot(up_xy, dot(x.T, up_z))
        for j in range(32):
            e1[c, j + 1] = lifted[16 * j : 16 * j + 16]
    plane_factors(mod1, 2.0, faces1, diag1, inv1, 1, 33, True)
    plane_sweep(e1, d1a, r1, r1w, faces1, diag1, inv1, 1, 33, START)
    for c in range(3):
        e1[c, 1:33] = e1[c, 1:33] + x1[c, 1:33] + d1a[c, 1:33]
    plane_sweep(d1a, d1b, r1w, r1w, faces1, diag1, inv1, 1, 33, CHEB[0])
    for c in range(3):
        e1[c, 1:33] = e1[c, 1:33] + d1b[c, 1:33]
    plane_sweep(d1b, d1a, r1w, None, faces1, diag1, inv1, 1, 33, CHEB[1])
    for c in range(3):
        e1[c, 1:33] = e1[c, 1:33] + d1a[c, 1:33]
    row = iota((24, 16), 0)
    row = jnp.where(row >= 16, row - 24, row)
    up_y = ones_where((row + 8 * gy + 16) // 2 - 8 == iota((24, 16), 1))
    up_z0 = ones_where(iota((128, 256), 1) // 2 == iota((128, 256), 0))
    for c in range(3):
        for j in range(8):
            at = jnp.clip(4 * gx + (j - 1), 0, 33)
            lifted = dot(dot(up_y, e1[c, at]), up_z0)
            d_b[c, 3 + 2 * j] = lifted
            d_b[c, 4 + 2 * j] = lifted
    plane_factors(mod0, 1.0, faces, diag, inv, 4, 19, False)
    own_part = (slice(7, 15), slice(0, 8), slice(0, 128))
    for c in range(3):
        disp[c] = x0[c] + d_b[(c,) + own_part]
    plane_sweep(d_b, d_a, r0, r_w, faces, diag, inv, 4, 18, START, 4, 0)
    for c in range(3):
        disp[c] = disp[c] + d_a[(c,) + own_part]
    plane_sweep(d_a, d_b, r_w, r_w, faces, diag, inv, 5, 17, CHEB[0])
    for c in range(3):
        disp[c] = disp[c] + d_b[(c,) + own_part]
    plane_sweep(d_b, d_a, r_w, r_w, faces, diag, inv, 6, 16, CHEB[1])
    for c in range(3):
        disp[c] = disp[c] + d_a[(c,) + own_part]
    plane_sweep(d_a, None, r_w, r_w, faces, diag, inv, 7, 15, None)
    for c in range(3):
        resid[c] = r_w[(c,) + own_part]


IN_VMEM = pl.BlockSpec(memory_space=pltpu.VMEM)
IN_SMEM = pl.BlockSpec(memory_space=pltpu.SMEM)


def shaped(*shape):
    return jax.ShapeDtypeStruct(shape, F32)


def scratch(*shape):
    return pltpu.VMEM(shape, F32)


PARAMS = dict(compiler_params=pltpu.CompilerParams(vmem_limit_bytes=VMEM_LIMIT))


def call_a(moduli, ext):
    return pl.pallas_call(
        kernel_a,
        out_shape=(shaped(96, 128), shaped(3, 14, 24, 256), shaped(3, 8, 8, 128), shaped(3, 22, 24, 256)),
        in_specs=[IN_SMEM, IN_VMEM],
        out_specs=(IN_VMEM,) * 4,
        scratch_shapes=[scratch(6, 22, 24, 256)] + [scratch(3, 22, 24, 256)] * 5,
        **PARAMS,
    )(moduli, ext)


def call_b(got):
    one, two = (3, 34, 16, 128), (3, 64, 128)
    return pl.pallas_call(
        kernel_b,
        out_shape=(shaped(2, 16, 128),) + (shaped(*one),) * 3 + (shaped(*two),) * 3,
        in_specs=[IN_VMEM],
        out_specs=(IN_VMEM,) * 7,
        scratch_shapes=[scratch(6, 34, 16, 128)] + [scratch(*one)] * 5,
        **PARAMS,
    )(got)


def call_c(place, got, level1, level2, level0):
    one, zero = (3, 34, 16, 128), (3, 22, 24, 256)
    return pl.pallas_call(
        kernel_c,
        out_shape=(shaped(3, 8, 8, 128), shaped(3, 8, 8, 128)),
        in_specs=[IN_SMEM] + [IN_VMEM] * 10,
        out_specs=(IN_VMEM,) * 2,
        scratch_shapes=[scratch(3, 16, 32, 128), scratch(272, 128), scratch(*one)]
        + [scratch(6, 34, 16, 128)] + [scratch(*one)] * 5
        + [scratch(6, 22, 24, 256)] + [scratch(*zero)] * 5,
        **PARAMS,
    )(place, got, *level1, *level2, *level0)


def both_ways(to_next, to_before, axis):
    count = lax.axis_size(axis)
    up = [(i, i + 1) for i in range(count - 1)]
    down = [(j, i) for i, j in up]
    return lax.ppermute(to_next, axis, up), lax.ppermute(to_before, axis, down)


def extend(body_forces, material, fixed_mask):
    cells = jnp.concatenate(
        [body_forces, (material + 1).astype(F32)[None], (1 - fixed_mask).astype(F32)[None]], axis=0
    )
    before, after = both_ways(cells, cells, "gz")
    halo = jnp.where(iota((1, 1, 1, 128), 3) < 64, after, before)
    cells = jnp.concatenate([cells, halo], axis=3)
    before, after = both_ways(cells[:, 1:8], cells[:, 0:7], "gx")
    cells = jnp.concatenate([before, cells, after], axis=1)
    before, after = both_ways(cells, cells, "gy")
    return jnp.concatenate([cells, after, before], axis=2)


def to_all(block, axes, count):
    copies = jnp.broadcast_to(block[None], (count,) + block.shape)
    return lax.all_to_all(copies, axes, 0, 0, tiled=True)


def body(body_forces, material, fixed_mask, moduli):
    ext = extend(body_forces, material, fixed_mask)
    send, r0, x0, mod0 = call_a(moduli, ext)
    send, mod1, x1, r1, mod2, x2, r2 = call_b(to_all(send, ("gx", "gy"), 32))
    got = to_all(send, "gz", 16)
    place = jnp.stack([lax.axis_index("gx"), lax.axis_index("gy"), lax.axis_index("gz")]).astype(jnp.int32)
    return call_c(place, got, (mod1, x1, r1), (mod2, x2, r2), (mod0, x0, r0))


def solution(mesh):
    cells = P(None, "gx", "gy", "gz")
    part = P("gx", "gy", "gz")
    return jax.shard_map(
        body, mesh=mesh, in_specs=(cells, part, part, P()), out_specs=(cells, cells), check_vma=False
    )
```

time: 1490 us -> 213 us (0.14)
  the two profiles are of different devices: /device:TPU:224 before, /device:TPU:1 now
where the time goes in v1:
time: 213 us
  Pallas kernels  85.9 us (40%)
  blocking collectives  50.3 us (24%)
  waiting for transfers between devices  41.3 us (19%)
  starting transfers between devices  26.5 us (12%)
  other arithmetic  4.56 us (2%)
  local copies, waits for them, and re-layouts  3.13 us (1%)
    pallas_call x1, Pallas kernels, call_c(): pl.pallas_call(kernel_c, out_shape=(shaped(3, 8, 8, 128), shaped(3, 8, 8,...  56.8 us
    all_to_all x1, blocking collectives, to_all(): return lax.all_to_all(copies, axes, 0, 0, tiled=True)  50.3 us
    ppermute x3, waiting for transfers between devices, both_ways(): lax.ppermute(to_before, axis, down)  21.9 us
    pallas_call x1, Pallas kernels, call_b(): pl.pallas_call(kernel_b, out_shape=(shaped(2, 16, 128),) + (shaped(*one),...  17.2 us
    pallas_call x1, Pallas kernels, call_a(): pl.pallas_call(kernel_a, out_shape=(shaped(96, 128), shaped(3, 14, 24, 25...  11.9 us
    all_to_all x1, waiting for transfers between devices, to_all(): return lax.all_to_all(copies, axes, 0, 0, tiled=True)  11.6 us
    ppermute x3, starting transfers between devices, both_ways(): lax.ppermute(to_before, axis, down)  11.4 us
    all_to_all x1, starting transfers between devices, to_all(): return lax.all_to_all(copies, axes, 0, 0, tiled=True)  7.9 us
  transfers between devices with their start and end apart: 7, of which 6 were waited for; matrix products, arithmetic and copies ran while one was open for 0% of the time, Pallas kernels for 0%

profile of v1, /device:TPU:1, one launch (start us, length us, event | category | flops | bytes accessed | tf_op | source)
XLA Modules:
  0.0 212.6 jit_solution(18434691613630264867)
XLA Ops:
  0.6 0.0 copy-start.3
  0.6 0.8 convert_bitcast_fusion
  1.5 0.9 pad_maximum_fusion.3
  2.4 8.8 %collective-permute-start = (f32[5,8,8,128]{3,2,1,0:T(8,128)S(1)}, f32[5,8,8,128]{3,2,1,0:T(8,128)S(1)}, u32[]{:S(2)}, u32[]{:S(2)}) collective-permute-start(f32[5,8,8,128]{3,2,1,0:T(8,128)S(1)} %pad_maximum_fusion.3), channel_id=1, source_target_pairs={{1,0},{2,1},{3,2},{4,3},{5,4},{6,5},{7,6},{8,7},{9,8},{10,9},{11,1... | collective-permute-start | bytes 491528 | tf_op jit(solution)/shard_map/ppermute | solution.py:555
  11.2 1.9 collective-permute-start.1
  13.1 0.0 collective-permute-done
  13.1 2.2 %collective-permute-done.1 = f32[5,8,8,128]{3,2,1,0:T(8,128)S(1)} collective-permute-done((f32[5,8,8,128]{3,2,1,0:T(8,128)S(1)}, f32[5,8,8,128]{3,2,1,0:T(8,128)S(1)}, u32[]{:S(2)}, u32[]{:S(2)}) %collective-permute-start.1) | collective-permute-done | bytes 163872 | tf_op jit(solution)/shard_map/ppermute | solution.py:555
  15.4 0.9 pad_maximum_fusion.2
  16.3 1.3 collective-permute-start.2
  17.6 1.3 collective-permute-start.3
  18.9 4.8 %collective-permute-done.2 = f32[5,7,8,256]{3,2,1,0:T(8,128)S(1)} collective-permute-done((f32[5,7,8,256]{3,2,1,0:T(8,128)S(1)}, f32[5,7,8,256]{3,2,1,0:T(8,128)S(1)}, u32[]{:S(2)}, u32[]{:S(2)}) %collective-permute-start.2) | collective-permute-done | bytes 286752 | tf_op jit(solution)/shard_map/ppermute | solution.py:555
  23.7 4.1 %collective-permute-done.3 = f32[5,7,8,256]{3,2,1,0:T(8,128)S(1)} collective-permute-done((f32[5,7,8,256]{3,2,1,0:T(8,128)S(1)}, f32[5,7,8,256]{3,2,1,0:T(8,128)S(1)}, u32[]{:S(2)}, u32[]{:S(2)}) %collective-permute-start.3) | collective-permute-done | bytes 286752 | tf_op jit(solution)/shard_map/ppermute | solution.py:555
  27.8 0.0 copy-done.3
  27.8 0.1 pad_maximum_fusion.1
  27.9 0.0 copy-start.2
  27.9 1.3 collective-permute-start.4
  29.2 4.0 %collective-permute-start.5 = (f32[5,22,8,256]{3,2,1,0:T(8,128)S(1)}, f32[5,22,8,256]{3,2,1,0:T(8,128)S(1)}, u32[]{:S(2)}, u32[]{:S(2)}) collective-permute-start(f32[5,22,8,256]{3,2,1,0:T(8,128)S(1)} %pad_maximum_fusion.1), channel_id=1, source_target_pairs={{0,16},{16,32},{32,48},{1,17},{17,33},{33,49},{2,18},{18,34},{34,5... | collective-permute-start | bytes 2703368 | tf_op jit(solution)/shard_map/ppermute | solution.py:555
  33.3 17.7 %collective-permute-done.4 = f32[5,22,8,256]{3,2,1,0:T(8,128)S(1)} collective-permute-done((f32[5,22,8,256]{3,2,1,0:T(8,128)S(1)}, f32[5,22,8,256]{3,2,1,0:T(8,128)S(1)}, u32[]{:S(2)}, u32[]{:S(2)}) %collective-permute-start.4) | collective-permute-done | bytes 901152 | tf_op jit(solution)/shard_map/ppermute | solution.py:555
  51.0 0.9 collective-permute-done.5
  51.9 1.8 pad_maximum_fusion.ext
  53.6 0.0 copy-done.2
  53.6 11.9 %shard_map.59 = (f32[96,128]{1,0:T(8,128)S(1)}, f32[3,14,24,256]{3,2,1,0:T(8,128)S(1)}, f32[3,8,8,128]{3,2,1,0:T(8,128)S(1)}, f32[3,22,24,256]{3,2,1,0:T(8,128)S(1)}) custom-call(f32[2,16]{1,0:T(2,128)S(1)} %copy-done.2, f32[5,22,24,256]{3,2,1,0:T(8,128)} %pad_maximum_fusion.ext), custom_call_target="tpu_custom_call" | custom-call | tf_op jit(solution)/shard_map/pallas_call | solution.py:515
  65.5 0.0 copy-start
  65.5 1.2 copy-done
  66.7 0.0 copy-start.1
  66.7 1.0 copy-done.1
  67.7 0.2 broadcast_in_dim.29
  67.9 50.3 %all_to_all.10.got = f32[32,96,128]{2,1,0:T(8,128)} all-to-all(f32[32,96,128]{2,1,0:T(8,128)S(1)} %broadcast_in_dim.29), channel_id=1, replica_groups=mesh['gx'=8,'gy'=4,'gz'=16] {'gx','gy'}, dimensions={0} | all-to-all | bytes 3145728 | tf_op jit(solution)/shard_map/all_to_all | solution.py:573
  118.2 17.2 %shard_map.60 = (f32[2,16,128]{2,1,0:T(8,128)S(1)}, f32[3,34,16,128]{3,2,1,0:T(8,128)S(1)}, f32[3,34,16,128]{3,2,1,0:T(8,128)S(1)}, f32[3,34,16,128]{3,2,1,0:T(8...) custom-call(f32[32,96,128]{2,1,0:T(8,128)} %all_to_all.10.got), custom_call_target="tpu_custom_call" | custom-call | tf_op jit(solution)/shard_map/pallas_call | solution.py:527
  135.4 0.7 broadcast_in_dim.30
  136.2 7.9 %all-to-all-start.1 = ((f32[16,2,16,128]{3,2,1,0:T(8,128)}), f32[16,2,16,128]{3,2,1,0:T(8,128)S(1)}, u32[]{:S(2)}, u32[]{:S(2)}) async-start(f32[16,2,16,128]{3,2,1,0:T(8,128)} %broadcast_in_dim.30), calls=%async_computation.1 | async-start | bytes 524288 | tf_op jit(solution)/shard_map/all_to_all | solution.py:573
  144.1 0.1 pad_add_fusion.place
  144.1 11.6 %all-to-all-done.1.got = f32[16,2,16,128]{3,2,1,0:T(8,128)S(1)} async-done(((f32[16,2,16,128]{3,2,1,0:T(8,128)}), f32[16,2,16,128]{3,2,1,0:T(8,128)S(1)}, u32[]{:S(2)}, u32[]{:S(2)}) %all-to-all-start.1) | async-done | bytes 262176 | tf_op jit(solution)/shard_map/all_to_all | solution.py:573
  155.8 56.8 %shard_map.61 = (f32[3,8,8,128]{3,2,1,0:T(8,128)}, f32[3,8,8,128]{3,2,1,0:T(8,128)}) custom-call(s32[3]{0:T(128)S(1)} %pad_add_fusion.place, f32[16,2,16,128]{3,2,1,0:T(8,128)S(1)} %all-to-all-done.1.got, f32[3,34,16,128]{3,2,1,0:T(8,128)S(1)} %get-tuple-element.15.mod1, f32[3,34,16,128]{3,2,1,0:T(8,128)S(1)} %get-tuple-element.16.x1, ...), custom_call_target="tpu_custom_call" | custom-call | tf_op jit(solution)/shard_map/pallas_call | solution.py:539
  (3 shorter events, 0.1 us)
Async XLA Ops:
  0.6 27.2 %copy-start.3 = (f32[3,8,8,128]{3,2,1,0:T(8,128)S(1)}, f32[3,8,8,128]{3,2,1,0:T(8,128)}, u32[]{:S(2)}) copy-start(f32[3,8,8,128]{3,2,1,0:T(8,128)} %param.4) | copy-start | bytes 294916
  2.4 10.7 %collective-permute-start = (f32[5,8,8,128]{3,2,1,0:T(8,128)S(1)}, f32[5,8,8,128]{3,2,1,0:T(8,128)S(1)}, u32[]{:S(2)}, u32[]{:S(2)}) collective-permute-start(f32[5,8,8,128]{3,2,1,0:T(8,128)S(1)} %pad_maximum_fusion.3), channel_id=1, source_target_pairs={{1,0},{2,1},{3,2},{4,3},{5,4},{6,5},{7,6},{8,7},{9,8},{10,9},{11,1... | collective-permute-start | bytes 491528 | tf_op jit(solution)/shard_map/ppermute | solution.py:555
  11.2 4.2 %collective-permute-start.1 = (f32[5,8,8,128]{3,2,1,0:T(8,128)S(1)}, f32[5,8,8,128]{3,2,1,0:T(8,128)S(1)}, u32[]{:S(2)}, u32[]{:S(2)}) collective-permute-start(f32[5,8,8,128]{3,2,1,0:T(8,128)S(1)} %pad_maximum_fusion.3), channel_id=1, source_target_pairs={{0,1},{1,2},{2,3},{3,4},{4,5},{5,6},{6,7},{7,8},{8,9},{9,10},{10,1... | collective-permute-start | bytes 491528 | tf_op jit(solution)/shard_map/ppermute | solution.py:555
  16.3 7.4 %collective-permute-start.2 = (f32[5,7,8,256]{3,2,1,0:T(8,128)S(1)}, f32[5,7,8,256]{3,2,1,0:T(8,128)S(1)}, u32[]{:S(2)}, u32[]{:S(2)}) collective-permute-start(f32[5,7,8,256]{3,2,1,0:T(8,128)S(1)} %get-tuple-element.24), channel_id=1, source_target_pairs={{0,64},{64,128},{128,192},{192,256},{256,320},{320,384},{384,448},... | collective-permute-start | bytes 860168 | tf_op jit(solution)/shard_map/ppermute | solution.py:555
  17.6 10.2 %collective-permute-start.3 = (f32[5,7,8,256]{3,2,1,0:T(8,128)S(1)}, f32[5,7,8,256]{3,2,1,0:T(8,128)S(1)}, u32[]{:S(2)}, u32[]{:S(2)}) collective-permute-start(f32[5,7,8,256]{3,2,1,0:T(8,128)S(1)} %get-tuple-element.25), channel_id=1, source_target_pairs={{64,0},{128,64},{192,128},{256,192},{320,256},{384,320},{448,384},... | collective-permute-start | bytes 860168 | tf_op jit(solution)/shard_map/ppermute | solution.py:555
  27.9 25.7 %copy-start.2 = (f32[2,16]{1,0:T(2,128)S(1)}, f32[2,16]{1,0:T(2,128)}, u32[]{:S(2)}) copy-start(f32[2,16]{1,0:T(2,128)} %moduli.1) | copy-start | bytes 388
  27.9 23.1 %collective-permute-start.4 = (f32[5,22,8,256]{3,2,1,0:T(8,128)S(1)}, f32[5,22,8,256]{3,2,1,0:T(8,128)S(1)}, u32[]{:S(2)}, u32[]{:S(2)}) collective-permute-start(f32[5,22,8,256]{3,2,1,0:T(8,128)S(1)} %pad_maximum_fusion.1), channel_id=1, source_target_pairs={{16,0},{32,16},{48,32},{17,1},{33,17},{49,33},{18,2},{34,18},{50,3... | collective-permute-start | bytes 2703368 | tf_op jit(solution)/shard_map/ppermute | solution.py:555
  29.2 22.6 %collective-permute-start.5 = (f32[5,22,8,256]{3,2,1,0:T(8,128)S(1)}, f32[5,22,8,256]{3,2,1,0:T(8,128)S(1)}, u32[]{:S(2)}, u32[]{:S(2)}) collective-permute-start(f32[5,22,8,256]{3,2,1,0:T(8,128)S(1)} %pad_maximum_fusion.1), channel_id=1, source_target_pairs={{0,16},{16,32},{32,48},{1,17},{17,33},{33,49},{2,18},{18,34},{34,5... | collective-permute-start | bytes 2703368 | tf_op jit(solution)/shard_map/ppermute | solution.py:555
  65.5 1.2 copy-start
  66.7 1.0 copy-start.1
  136.2 19.6 %all-to-all-start.1 = ((f32[16,2,16,128]{3,2,1,0:T(8,128)}), f32[16,2,16,128]{3,2,1,0:T(8,128)S(1)}, u32[]{:S(2)}, u32[]{:S(2)}) async-start(f32[16,2,16,128]{3,2,1,0:T(8,128)} %broadcast_in_dim.30), calls=%async_computation.1 | async-start | bytes 524288 | tf_op jit(solution)/shard_map/all_to_all | solution.py:573

commit v2 on v1

--- a/solution.py
+++ b/solution.py
@@ -10,7 +10,7 @@
 THETA = 1.125
 HALF = 0.875
 SIGMA = THETA / HALF
-VMEM_LIMIT = 50 * 1024 * 1024
+VMEM_LIMIT = 28 * 1024 * 1024
 
 
 def cheb_factors():
@@ -27,16 +27,40 @@
 START = (0.0, 1.0 / THETA)
 
 
-def dot(a, b):
-    return lax.dot_general(
-        a, b, (((1,), (0,)), ((), ())), precision=lax.Precision.HIGHEST, preferred_element_type=F32
-    )
-
-
-def dot_nt(a, b):
-    return lax.dot_general(
-        a, b, (((1,), (1,)), ((), ())), precision=lax.Precision.HIGHEST, preferred_element_type=F32
-    )
+BF16 = jnp.bfloat16
+
+
+def split(v):
+    high = v.astype(BF16)
+    return high, (v - high.astype(F32)).astype(BF16)
+
+
+def mxu(a, b, b_dim=0):
+    return lax.dot_general(a, b, (((1,), (b_dim,)), ((), ())), preferred_element_type=F32)
+
+
+def dot_l(picks, v):
+    high, low = split(v)
+    picks = picks.astype(BF16)
+    return mxu(picks, high) + mxu(picks, low)
+
+
+def dot_r(v, picks):
+    high, low = split(v)
+    picks = picks.astype(BF16)
+    return mxu(high, picks) + mxu(low, picks)
+
+
+def dot_l_nt(picks, v):
+    high, low = split(v)
+    picks = picks.astype(BF16)
+    return mxu(picks, high, 1) + mxu(picks, low, 1)
+
+
+def dot_r_nt(v, picks):
+    high, low = split(v)
+    picks = picks.astype(BF16)
+    return mxu(high, picks, 1) + mxu(low, picks, 1)
 
 
 def iota(shape, dim):
@@ -50,6 +74,18 @@
 def roll(v, shift, axis):
     size = v.shape[axis]
     return pltpu.roll(v, shift % size, axis)
+
+
+def loop(lo, hi, body):
+    count = hi - lo
+    step = max(k for k in (1, 2, 3, 4, 5) if count % k == 0)
+
+    def several(n, carry):
+        for k in range(step):
+            body(lo + n * step + k)
+        return carry
+
+    lax.fori_loop(0, count // step, several, 0)
 
 
 def neighbours_y(v, rows_masked):
@@ -64,7 +100,7 @@
 def plane_factors(mod, scale, faces, diag, inv, lo, hi, rows_masked):
     half = 0.5 * scale
 
-    def body(i, carry):
+    def body(i):
         def fields(j):
             shear, lame = mod[0, j], mod[1, j]
             return half * shear, half * (shear + lame)
@@ -90,13 +126,12 @@
             face = p + pn
             faces[2 * k, i] = both * face
             faces[2 * k + 1, i] = both * (face + (g + gn))
-        return carry
-
-    lax.fori_loop(lo, hi, body, 0)
+
+    loop(lo, hi, body)
 
 
 def plane_sweep(d, d_next, r_in, r_out, faces, diag, inv, lo, hi, pair, r_in_at=0, r_out_at=0):
-    def body(i, carry):
+    def body(i):
         for c in range(3):
             fx = faces[1 if c == 0 else 0, i]
             fxu = faces[1 if c == 0 else 0, i + 1]
@@ -114,13 +149,12 @@
                 if pair[0] != 0.0:
                     new = new + pair[0] * dc
                 d_next[c, i] = new
-        return carry
-
-    lax.fori_loop(lo, hi, body, 0)
+
+    loop(lo, hi, body)
 
 
 def kernel_a(moduli, ext, send, r_out, x_out, mod, faces, diag, inv, d_a, d_b, r):
-    def look_up(i, carry):
+    def look_up(i):
         mat = ext[3, i]
         shear = jnp.zeros(mat.shape, F32)
         lame = jnp.zeros(mat.shape, F32)
@@ -131,17 +165,15 @@
         mod[0, i] = shear
         mod[1, i] = lame
         mod[2, i] = ext[4, i]
-        return carry
-
-    lax.fori_loop(0, 22, look_up, 0)
+
+    loop(0, 22, look_up)
     plane_factors(mod, 1.0, faces, diag, inv, 1, 21, False)
 
-    def start(i, carry):
+    def start(i):
         for c in range(3):
             d_a[c, i] = (START[1] * inv[c, i]) * ext[c, i]
-        return carry
-
-    lax.fori_loop(1, 21, start, 0)
+
+    loop(1, 21, start)
     plane_sweep(d_a, d_b, ext, r, faces, diag, inv, 2, 20, CHEB[0])
     for c in range(3):
         x_out[c] = d_a[c, 7:15, 0:8, 0:128] + d_b[c, 7:15, 0:8, 0:128]
@@ -159,10 +191,18 @@
     stacked = jnp.concatenate(rows, axis=0)
     pair_z = ones_where(iota((256, 128), 0) // 2 == iota((256, 128), 1))
     pair_y = ones_where(iota((96, 192), 1) // 2 == iota((96, 192), 0))
-    low = dot(pair_y, dot(stacked, pair_z))
+    low = dot_l(pair_y, dot_r(stacked, pair_z))
     row = iota((96, 128), 0)
     low = jnp.where(row < 48, low, jnp.where(row < 80, 0.125 * low, ones_where(low > 0.5)))
-    send[...] = low
+    lane = iota((48, 128), 1)
+    send[0:48] = jnp.where(lane < 64, low[0:48], roll(low[48:96], 64, 1))
+    lane = iota((32, 128), 1)
+    packed = jnp.zeros((32, 128), F32)
+    for k in range(3):
+        part = low[32 * k : 32 * k + 32]
+        packed = jnp.where((lane >= 40 * k) & (lane < 40 * k + 20), roll(part, 40 * k - 64, 1), packed)
+        packed = jnp.where((lane >= 40 * k + 20) & (lane < 40 * k + 40), roll(part, 40 * k - 88, 1), packed)
+    send[48:80] = packed
 
 
 def flat_factors(mods, steps, scales, groups):
@@ -248,13 +288,25 @@
     for k in range(6):
         faces[k, 33] = zero
 
+    lane = iota((8, 128), 1)
+
+    def tile(dev, t):
+        own = got[dev, 8 * (t % 6) : 8 * (t % 6) + 8]
+        if t >= 6:
+            own = roll(own, 64, 1)
+        halo = got[dev, 48 + 8 * (t % 4) : 56 + 8 * (t % 4)]
+        after = roll(halo, 64 - 40 * (t // 4), 1)
+        before = roll(halo, 88 - 40 * (t // 4), 1)
+        halo = jnp.where(lane < 84, after, jnp.where(lane >= 108, before, 0.0))
+        return jnp.where(lane < 64, own, halo)
+
     def unpack(gx, carry):
         for f in range(6):
             for pair in range(2):
-                at = f * 16 + pair * 8
+                at = f * 2 + pair
                 for half in range(2):
-                    s0 = got[gx * 4 + 2 * half, at : at + 8]
-                    s1 = got[gx * 4 + 2 * half + 1, at : at + 8]
+                    s0 = tile(gx * 4 + 2 * half, at)
+                    s1 = tile(gx * 4 + 2 * half + 1, at)
                     even = jnp.where(sub, s0, roll(s1, 4, 0))
                     odd = jnp.where(sub, roll(s0, 4, 0), s1)
                     x = gx * 4 + 2 * pair + 1
@@ -270,12 +322,11 @@
     lax.fori_loop(0, 8, unpack, 0)
     plane_factors(mod1, 2.0, faces, diag, inv, 1, 33, True)
 
-    def start(i, carry):
+    def start(i):
         for c in range(3):
             d_a[c, i] = (START[1] * inv[c, i]) * b1[c, i]
-        return carry
-
-    lax.fori_loop(1, 33, start, 0)
+
+    loop(1, 33, start)
     plane_sweep(d_a, d_b, b1, r1, faces, diag, inv, 1, 33, CHEB[0])
     for c in range(3):
         x1[c] = d_a[c] + d_b[c]
@@ -289,7 +340,7 @@
 
     def restrict(ref, k):
         planes = [ref[k, 1 + 2 * j] + ref[k, 2 + 2 * j] for j in range(16)]
-        return dot_nt(pair_z, dot(pair_y, jnp.concatenate(planes, axis=0)))
+        return dot_l_nt(pair_z, dot_l(pair_y, jnp.concatenate(planes, axis=0)))
 
     shear = 0.125 * restrict(mod1, 0)
     lame = 0.125 * restrict(mod1, 1)
@@ -306,12 +357,12 @@
         x, r = flat_smooth(None, restrict(r1, c), factors, steps, True)
         x2[c] = x
         r2[c] = r
-        low = low + dot(dot(own_z, r), to_level3(c))
+        low = low + dot_r(dot_l(own_z, r), to_level3(c))
     send[0] = low
     lane = iota((16, 128), 1)
-    low = dot(dot(own_z, shear), to_level3(0)) + dot(dot(own_z, lame), to_level3(1))
+    low = dot_r(dot_l(own_z, shear), to_level3(0)) + dot_r(dot_l(own_z, lame), to_level3(1))
     low = 0.125 * low
-    low = low + ones_where(dot(dot(own_z, active), to_level3(2)) > 0.5)
+    low = low + ones_where(dot_r(dot_l(own_z, active), to_level3(2)) > 0.5)
     send[1] = low
 
 
@@ -322,59 +373,72 @@
     return back + roll(back, 32, 1) + roll(back, 64, 1)
 
 
+def eliminate(mat, cells):
+    tiles = [jnp.stack([mat[c, k, 8 * t : 8 * t + 8] for c, k in cells]) for t in range(4)]
+    rows = iota(tiles[0].shape, 1)
+    for p in range(0, 32, 2):
+        at, q = divmod(p, 8)
+        row0, row1 = tiles[at][:, q : q + 1, :], tiles[at][:, q + 1 : q + 2, :]
+        a00, a01 = row0[:, :, p : p + 1], row0[:, :, p + 1 : p + 2]
+        a10, a11 = row1[:, :, p : p + 1], row1[:, :, p + 1 : p + 2]
+        scale = 1.0 / (a00 * a11 - a01 * a10)
+        new0 = (a11 * scale) * row0 - (a01 * scale) * row1
+        new1 = (a00 * scale) * row1 - (a10 * scale) * row0
+        for t in range(4):
+            a = tiles[t]
+            a = a - (a[:, :, p : p + 1] * new0 + a[:, :, p + 1 : p + 2] * new1)
+            if t == at:
+                a = jnp.where(rows == q, new0, jnp.where(rows == q + 1, new1, a))
+            tiles[t] = a
+    for n, (c, k) in enumerate(cells):
+        for t in range(4):
+            mat[c, k, 8 * t : 8 * t + 8] = tiles[t][n]
+
+
 def coarse_solve(mods3, rest, mat):
     blocks = ones_where(iota((16, 256), 1) // 16 == iota((16, 256), 0))
-    shear = 0.0625 * dot(blocks, mods3[0])
-    lame = 0.0625 * dot(blocks, mods3[1])
-    active = ones_where(dot(blocks, mods3[2]) > 0.5)
-    side = dot(blocks, rest)
+    shear = 0.0625 * dot_l(blocks, mods3[0])
+    lame = 0.0625 * dot_l(blocks, mods3[1])
+    active = ones_where(dot_l(blocks, mods3[2]) > 0.5)
+    side = dot_l(blocks, rest)
     steps = level3_steps(16)
     scales = (128.0, 128.0, 0.5)
     faces, diag, _ = flat_factors((shear, lame, active), steps, scales, level3_groups(16))
-    columns = [diag, side]
+    uppers = []
     for face, (axis, shift, below, above) in zip(faces, steps):
-        columns.append(face)
-        columns.append(jnp.where(above, roll(face, -shift, axis), 0.0))
-    stacked = jnp.concatenate(columns, axis=0).T
+        uppers.append(jnp.where(above, roll(face, -shift, axis), 0.0))
+    lane16 = iota((16, 128), 1)
     row = iota((32, 128), 0)
     lane = iota((32, 128), 1)
-    patterns = (
-        ones_where(lane == row),
-        ones_where(lane == 96),
-        -ones_where((lane == row - 4) & (lane < 32)),
-        -ones_where((lane == row + 4) & (lane < 32)),
-        -ones_where((lane == row - 1) & (lane < 32)),
-        -ones_where((lane == row + 1) & (lane < 32)),
-        -ones_where(lane == row + 32),
-        -ones_where(lane == row + 64),
-    )
-    for c in range(3):
-        part = stacked[32 * c : 32 * c + 32]
+    at_diag = lane % 32 == row
+    inner = lane < 32
+    patterns = (inner & (lane == row - 4), inner & (lane == row + 4), inner & (lane == row - 1), inner & (lane == row + 1))
+    columns = jnp.concatenate([faces[2], uppers[2]] + [jnp.zeros((16, 128), F32)] * 6, axis=0).T
+    for c in range(3):
+        first = jnp.where(
+            lane16 < 32,
+            roll(diag, -32 * c, 1),
+            jnp.where(
+                lane16 < 64,
+                -roll(faces[2], 32 - 32 * c, 1),
+                jnp.where(lane16 < 96, -roll(uppers[2], 64 - 32 * c, 1), roll(side, 96 - 32 * c, 1)),
+            ),
+        )
+        others = [-roll(v, -32 * c, 1) for v in (uppers[0], faces[0], uppers[1], faces[1])]
         for k in range(16):
-            m = 0.0
-            for q in range(8):
-                at = 16 * q + k
-                m = m + part[:, at : at + 1] * patterns[q]
+            m = jnp.where(at_diag, first[k : k + 1], 0.0)
+            for pattern, v in zip(patterns, others):
+                m = jnp.where(pattern, v[k : k + 1], m)
             mat[c, k] = m
 
-    def eliminate(cells):
-        a = jnp.stack([mat[c, k] for c, k in cells])
-        rows = iota(a.shape, 1)
-        for p in range(32):
-            pivot = a[:, p : p + 1, :]
-            pivot = pivot * (1.0 / a[:, p : p + 1, p : p + 1])
-            a = jnp.where(rows == p, pivot, a - a[:, :, p : p + 1] * pivot)
-        for n, (c, k) in enumerate(cells):
-            mat[c, k] = a[n]
-
-    lane_t = lane < 32
+    lane_t = inner
     lane_l = (lane >= 32) & (lane < 64)
     lane_r = (lane >= 64) & (lane < 96)
     lane_b = lane >= 96
     keep = lane_t | lane_b
     none = jnp.zeros((32, 128), F32)
     for h in (1, 2, 4, 8):
-        eliminate([(c, k) for c in range(3) for k in range(h, 16, 2 * h)])
+        eliminate(mat, [(c, k) for c in range(3) for k in range(h, 16, 2 * h)])
         for c in range(3):
             for k in range(0, 16, 2 * h):
                 m = mat[c, k]
@@ -385,29 +449,41 @@
                 if k + h < 16:
                     w = mat[c, k + h]
                     right = jnp.where(lane_t, roll(w, 96, 1), jnp.where(lane_r | lane_b, w, 0.0))
-                change = dot(m, jnp.concatenate([none, left, right, none], axis=0))
+                if h == 1:
+                    part = columns[32 * c : 32 * c + 32]
+                    change = -(part[:, k : k + 1] * left + part[:, 16 + k : 17 + k] * right)
+                else:
+                    high, low = split(roll(m, -32, 1))
+                    both = jnp.where(lane < 64, high.astype(F32), roll(low.astype(F32), 64, 1)).astype(BF16)
+                    w_high, w_low = split(jnp.concatenate([left, right], axis=0))
+                    change = mxu(
+                        jnp.concatenate([both, both], axis=1),
+                        jnp.concatenate([w_high, w_high, w_low, w_low], axis=0),
+                    )
                 mat[c, k] = jnp.where(keep, m, 0.0) - change
-    eliminate([(c, 0) for c in range(3)])
-    picked = lane == 96
-    first_row = ones_where(row == 0)
+    eliminate(mat, [(c, 0) for c in range(3)])
     pieces = []
-    for c in range(3):
-        found = {}
-        last = jnp.where(picked, mat[c, 0], 0.0)
-        found[0] = jnp.broadcast_to(jnp.sum(last, axis=1, keepdims=True), (32, 128))
-        for h in (8, 4, 2, 1):
+    found = {}
+    for c in range(3):
+        found[c, 0] = jnp.sum(jnp.where(lane_b, mat[c, 0], 0.0), axis=1, keepdims=True)
+    for h in (8, 4, 2, 1):
+        for c in range(3):
             for k in range(h, 16, 2 * h):
-                after = -found[k + h] if k + h < 16 else none
-                v = jnp.concatenate([none, -found[k - h], after, first_row], axis=0)
-                found[k] = dot(mat[c, k], v)
+                v = jnp.where(lane_l & at_diag, -found[c, k - h], 0.0)
+                if k + h < 16:
+                    v = jnp.where(lane_r & at_diag, -found[c, k + h], v)
+                v = jnp.sum(v, axis=0, keepdims=True)
+                v = jnp.where(lane_b[0:1], 1.0, v)
+                found[c, k] = jnp.sum(mat[c, k] * v, axis=1, keepdims=True)
+    for c in range(3):
         piece = none
         for k in range(16):
-            piece = jnp.where(lane == k, found[k], piece)
+            piece = jnp.where(lane == k, found[c, k], piece)
         pieces.append(piece)
     pieces.append(none)
     whole = jnp.concatenate(pieces, axis=0)
     again = ones_where(iota((256, 128), 0) // 16 == iota((256, 128), 1))
-    return dot_nt(again, whole)
+    return dot_l_nt(again, whole)
 
 
 def kernel_c(
@@ -432,7 +508,7 @@
     own = e3[pl.ds(base + 8, 24)]
     before = e3[pl.ds(base, 8)]
     slab = jnp.concatenate([own, before], axis=0)
-    slab = dot(ones_where(iota((64, 32), 0) // 2 == iota((64, 32), 1)), slab)
+    slab = dot_l(ones_where(iota((64, 32), 0) // 2 == iota((64, 32), 1)), slab)
     steps = level2_steps()
     mods = (mod2[0], mod2[1], mod2[2])
     for k in range(3):
@@ -451,11 +527,11 @@
     for c in range(3):
         shares = tuple(1.0 if c == k else 0.0 for k in range(3))
         factors = flat_factors(mods, steps, (4.0, 4.0, 4.0), shares)
-        corr = dot_nt(slab, to_level3(c))
+        corr = dot_r_nt(slab, to_level3(c))
         x = x2[c] + corr
         r = r2[c] - flat_apply(corr, factors, steps)
         x, _ = flat_smooth(x, r, factors, steps, False)
-        lifted = dot(up_xy, dot(x.T, up_z))
+        lifted = dot_l(up_xy, dot_r(x.T, up_z))
         for j in range(32):
             e1[c, j + 1] = lifted[16 * j : 16 * j + 16]
     plane_factors(mod1, 2.0, faces1, diag1, inv1, 1, 33, True)
@@ -472,12 +548,19 @@
     row = jnp.where(row >= 16, row - 24, row)
     up_y = ones_where((row + 8 * gy + 16) // 2 - 8 == iota((24, 16), 1))
     up_z0 = ones_where(iota((128, 256), 1) // 2 == iota((128, 256), 0))
+    planes = []
     for c in range(3):
         for j in range(8):
-            at = jnp.clip(4 * gx + (j - 1), 0, 33)
-            lifted = dot(dot(up_y, e1[c, at]), up_z0)
-            d_b[c, 3 + 2 * j] = lifted
-            d_b[c, 4 + 2 * j] = lifted
+            planes.append(e1[c, jnp.clip(4 * gx + (j - 1), 0, 33)])
+    lifted = dot_r(jnp.concatenate(planes, axis=0), up_z0)
+    up_y = jnp.concatenate([up_y, up_y], axis=1).astype(BF16)
+    for c in range(3):
+        for j in range(8):
+            at = 16 * (8 * c + j)
+            high, low = split(lifted[at : at + 16])
+            plane = mxu(up_y, jnp.concatenate([high, low], axis=0))
+            d_b[c, 3 + 2 * j] = plane
+            d_b[c, 4 + 2 * j] = plane
     plane_factors(mod0, 1.0, faces, diag, inv, 4, 19, False)
     own_part = (slice(7, 15), slice(0, 8), slice(0, 128))
     for c in range(3):
@@ -514,7 +597,7 @@
 def call_a(moduli, ext):
     return pl.pallas_call(
         kernel_a,
-        out_shape=(shaped(96, 128), shaped(3, 14, 24, 256), shaped(3, 8, 8, 128), shaped(3, 22, 24, 256)),
+        out_shape=(shaped(80, 128), shaped(3, 14, 24, 256), shaped(3, 8, 8, 128), shaped(3, 22, 24, 256)),
         in_specs=[IN_SMEM, IN_VMEM],
         out_specs=(IN_VMEM,) * 4,
         scratch_shapes=[scratch(6, 22, 24, 256)] + [scratch(3, 22, 24, 256)] * 5,

time: 213 us -> 190 us (0.89)
  Pallas kernels: 85.9 us -> 65.9 us
  blocking collectives: 50.3 us -> 45.4 us
  local copies, waits for them, and re-layouts: 3.13 us -> 7.11 us
    pallas_call x1, Pallas kernels: 17.2 us -> 8.54 us  [call_b(): pl.pallas_call(kernel_b, out_shape=(shaped(2, 16, 128),) + (shaped(*one),...]
    pallas_call x1, Pallas kernels: 56.8 us -> 49.9 us  [call_c(): pl.pallas_call(kernel_c, out_shape=(shaped(3, 8, 8, 128), shaped(3, 8, 8,...]
    all_to_all x1, blocking collectives: 50.3 us -> 45.4 us  [to_all(): return lax.all_to_all(copies, axes, 0, 0, tiled=True)]
    pallas_call x1, Pallas kernels: 11.9 us -> 7.46 us  [call_a(): pl.pallas_call(kernel_a, out_shape=(shaped(80, 128), shaped(3, 14, 24, 25...]
    unnamed x8 -> x16, local copies, waits for them, and re-layouts: 2.19 us -> 6.25 us
where the time goes in v2:
time: 190 us
  Pallas kernels  65.9 us (35%)
  blocking collectives  45.4 us (24%)
  waiting for transfers between devices  41.3 us (22%)
  starting transfers between devices  26.3 us (14%)
  local copies, waits for them, and re-layouts  7.11 us (4%)
  other arithmetic  3.03 us (2%)
    pallas_call x1, Pallas kernels, call_c(): pl.pallas_call(kernel_c, out_shape=(shaped(3, 8, 8, 128), shaped(3, 8, 8,...  49.9 us
    all_to_all x1, blocking collectives, to_all(): return lax.all_to_all(copies, axes, 0, 0, tiled=True)  45.4 us
    ppermute x3, waiting for transfers between devices, both_ways(): lax.ppermute(to_before, axis, down)  21.9 us
    all_to_all x1, waiting for transfers between devices, to_all(): return lax.all_to_all(copies, axes, 0, 0, tiled=True)  11.6 us
    ppermute x3, starting transfers between devices, both_ways(): lax.ppermute(to_before, axis, down)  11.4 us
    pallas_call x1, Pallas kernels, call_b(): pl.pallas_call(kernel_b, out_shape=(shaped(2, 16, 128),) + (shaped(*one),...  8.54 us
    ppermute x3, waiting for transfers between devices, both_ways(): lax.ppermute(to_next, axis, up)  7.84 us
    all_to_all x1, starting transfers between devices, to_all(): return lax.all_to_all(copies, axes, 0, 0, tiled=True)  7.66 us
  transfers between devices with their start and end apart: 7, of which 6 were waited for; matrix products, arithmetic and copies ran while one was open for 0% of the time, Pallas kernels for 0%

profile of v2, /device:TPU:1, one launch (start us, length us, event | category | flops | bytes accessed | tf_op | source)
XLA Modules:
  0.0 189.8 jit_solution(16460714186387141537)
XLA Ops:
  0.6 0.0 copy-start.7
  0.6 0.8 convert_bitcast_fusion
  1.5 0.9 pad_maximum_fusion.3
  2.4 8.8 %collective-permute-start = (f32[5,8,8,128]{3,2,1,0:T(8,128)S(1)}, f32[5,8,8,128]{3,2,1,0:T(8,128)S(1)}, u32[]{:S(2)}, u32[]{:S(2)}) collective-permute-start(f32[5,8,8,128]{3,2,1,0:T(8,128)S(1)} %pad_maximum_fusion.3), channel_id=1, source_target_pairs={{1,0},{2,1},{3,2},{4,3},{5,4},{6,5},{7,6},{8,7},{9,8},{10,9},{11,1... | collective-permute-start | bytes 491528 | tf_op jit(solution)/shard_map/ppermute | solution.py:638
  11.2 1.9 %collective-permute-start.1 = (f32[5,8,8,128]{3,2,1,0:T(8,128)S(1)}, f32[5,8,8,128]{3,2,1,0:T(8,128)S(1)}, u32[]{:S(2)}, u32[]{:S(2)}) collective-permute-start(f32[5,8,8,128]{3,2,1,0:T(8,128)S(1)} %pad_maximum_fusion.3), channel_id=1, source_target_pairs={{0,1},{1,2},{2,3},{3,4},{4,5},{5,6},{6,7},{7,8},{8,9},{9,10},{10,1... | collective-permute-start | bytes 491528 | tf_op jit(solution)/shard_map/ppermute | solution.py:638
  13.1 0.0 collective-permute-done
  13.1 2.2 %collective-permute-done.1 = f32[5,8,8,128]{3,2,1,0:T(8,128)S(1)} collective-permute-done((f32[5,8,8,128]{3,2,1,0:T(8,128)S(1)}, f32[5,8,8,128]{3,2,1,0:T(8,128)S(1)}, u32[]{:S(2)}, u32[]{:S(2)}) %collective-permute-start.1) | collective-permute-done | bytes 163872 | tf_op jit(solution)/shard_map/ppermute | solution.py:638
  15.4 0.9 pad_maximum_fusion.2
  16.3 1.3 collective-permute-start.2
  17.6 1.3 collective-permute-start.3
  18.9 4.8 %collective-permute-done.2 = f32[5,7,8,256]{3,2,1,0:T(8,128)S(1)} collective-permute-done((f32[5,7,8,256]{3,2,1,0:T(8,128)S(1)}, f32[5,7,8,256]{3,2,1,0:T(8,128)S(1)}, u32[]{:S(2)}, u32[]{:S(2)}) %collective-permute-start.2) | collective-permute-done | bytes 286752 | tf_op jit(solution)/shard_map/ppermute | solution.py:638
  23.7 4.1 %collective-permute-done.3 = f32[5,7,8,256]{3,2,1,0:T(8,128)S(1)} collective-permute-done((f32[5,7,8,256]{3,2,1,0:T(8,128)S(1)}, f32[5,7,8,256]{3,2,1,0:T(8,128)S(1)}, u32[]{:S(2)}, u32[]{:S(2)}) %collective-permute-start.3) | collective-permute-done | bytes 286752 | tf_op jit(solution)/shard_map/ppermute | solution.py:638
  27.8 0.0 copy-done.7
  27.8 0.1 pad_maximum_fusion.1
  27.9 0.0 copy-start.6
  27.9 1.3 collective-permute-start.4
  29.2 4.0 %collective-permute-start.5 = (f32[5,22,8,256]{3,2,1,0:T(8,128)S(1)}, f32[5,22,8,256]{3,2,1,0:T(8,128)S(1)}, u32[]{:S(2)}, u32[]{:S(2)}) collective-permute-start(f32[5,22,8,256]{3,2,1,0:T(8,128)S(1)} %pad_maximum_fusion.1), channel_id=1, source_target_pairs={{0,16},{16,32},{32,48},{1,17},{17,33},{33,49},{2,18},{18,34},{34,5... | collective-permute-start | bytes 2703368 | tf_op jit(solution)/shard_map/ppermute | solution.py:638
  33.3 17.7 %collective-permute-done.4 = f32[5,22,8,256]{3,2,1,0:T(8,128)S(1)} collective-permute-done((f32[5,22,8,256]{3,2,1,0:T(8,128)S(1)}, f32[5,22,8,256]{3,2,1,0:T(8,128)S(1)}, u32[]{:S(2)}, u32[]{:S(2)}) %collective-permute-start.4) | collective-permute-done | bytes 901152 | tf_op jit(solution)/shard_map/ppermute | solution.py:638
  51.0 0.9 collective-permute-done.5
  51.9 0.2 pad_maximum_fusion.ext
  52.1 0.0 copy-done.6
  52.1 7.5 %shard_map.59 = (f32[80,128]{1,0:T(8,128)S(1)}, f32[3,14,24,256]{3,2,1,0:T(8,128)S(1)}, f32[3,8,8,128]{3,2,1,0:T(8,128)S(1)}, f32[3,22,24,256]{3,2,1,0:T(8,128)S(1)}) custom-call(f32[2,16]{1,0:T(2,128)S(1)} %copy-done.6, f32[5,22,24,256]{3,2,1,0:T(8,128)S(1)} %pad_maximum_fusion.ext), custom_call_target="tpu_custom_call" | custom-call | tf_op jit(solution)/shard_map/pallas_call | solution.py:598
  59.6 0.1 broadcast_in_dim.29
  59.7 45.4 %all_to_all.10.got = f32[32,80,128]{2,1,0:T(8,128)S(1)} all-to-all(f32[32,80,128]{2,1,0:T(8,128)S(1)} %broadcast_in_dim.29), channel_id=1, replica_groups=mesh['gx'=8,'gy'=4,'gz'=16] {'gx','gy'}, dimensions={0} | all-to-all | bytes 2621440 | tf_op jit(solution)/shard_map/all_to_all | solution.py:656
  105.0 8.5 %shard_map.60 = (f32[2,16,128]{2,1,0:T(8,128)S(1)}, f32[3,34,16,128]{3,2,1,0:T(8,128)S(1)}, f32[3,34,16,128]{3,2,1,0:T(8,128)S(1)}, f32[3,34,16,128]{3,2,1,0:T(8...) custom-call(f32[32,80,128]{2,1,0:T(8,128)S(1)} %all_to_all.10.got), custom_call_target="tpu_custom_call" | custom-call | tf_op jit(solution)/shard_map/pallas_call | solution.py:610
  113.6 0.0 copy-start
  113.6 0.9 copy-done
  114.5 0.0 copy-start.2
  114.5 0.9 copy-done.2
  115.5 0.0 copy-start.4
  115.5 0.9 copy-done.4
  116.4 0.7 broadcast_in_dim.30
  117.1 7.7 %all-to-all-start.1 = ((f32[16,2,16,128]{3,2,1,0:T(8,128)}), f32[16,2,16,128]{3,2,1,0:T(8,128)S(1)}, u32[]{:S(2)}, u32[]{:S(2)}) async-start(f32[16,2,16,128]{3,2,1,0:T(8,128)} %broadcast_in_dim.30), calls=%async_computation.1 | async-start | bytes 524288 | tf_op jit(solution)/shard_map/all_to_all | solution.py:656
  124.8 0.1 pad_add_fusion.place
  124.8 11.6 %all-to-all-done.1.got = f32[16,2,16,128]{3,2,1,0:T(8,128)S(1)} async-done(((f32[16,2,16,128]{3,2,1,0:T(8,128)}), f32[16,2,16,128]{3,2,1,0:T(8,128)S(1)}, u32[]{:S(2)}, u32[]{:S(2)}) %all-to-all-start.1) | async-done | bytes 262176 | tf_op jit(solution)/shard_map/all_to_all | solution.py:656
  136.5 0.0 copy-start.1
  136.5 1.1 copy-done.1
  137.6 0.0 copy-start.3
  137.6 1.1 copy-done.3
  138.8 0.0 copy-start.5
  138.8 1.1 copy-done.5
  139.9 49.9 %shard_map.61 = (f32[3,8,8,128]{3,2,1,0:T(8,128)}, f32[3,8,8,128]{3,2,1,0:T(8,128)}) custom-call(s32[3]{0:T(128)S(1)} %pad_add_fusion.place, f32[16,2,16,128]{3,2,1,0:T(8,128)S(1)} %all-to-all-done.1.got, f32[3,34,16,128]{3,2,1,0:T(8,128)S(1)} %copy-done.1, f32[3,34,16,128]{3,2,1,0:T(8,128)S(1)} %copy-done.3, f32[3,34,16,128]{3,2,1,0:T(8,128)S(1)} %copy-done.5, ...), custom_call_target="tpu_custom_call" | custom-call | tf_op jit(solution)/shard_map/pallas_call | solution.py:622
  (3 shorter events, 0.1 us)
Async XLA Ops:
  0.6 27.2 %copy-start.7 = (f32[3,8,8,128]{3,2,1,0:T(8,128)S(1)}, f32[3,8,8,128]{3,2,1,0:T(8,128)}, u32[]{:S(2)}) copy-start(f32[3,8,8,128]{3,2,1,0:T(8,128)} %param.4) | copy-start | bytes 294916
  2.4 10.7 %collective-permute-start = (f32[5,8,8,128]{3,2,1,0:T(8,128)S(1)}, f32[5,8,8,128]{3,2,1,0:T(8,128)S(1)}, u32[]{:S(2)}, u32[]{:S(2)}) collective-permute-start(f32[5,8,8,128]{3,2,1,0:T(8,128)S(1)} %pad_maximum_fusion.3), channel_id=1, source_target_pairs={{1,0},{2,1},{3,2},{4,3},{5,4},{6,5},{7,6},{8,7},{9,8},{10,9},{11,1... | collective-permute-start | bytes 491528 | tf_op jit(solution)/shard_map/ppermute | solution.py:638
  11.2 4.2 %collective-permute-start.1 = (f32[5,8,8,128]{3,2,1,0:T(8,128)S(1)}, f32[5,8,8,128]{3,2,1,0:T(8,128)S(1)}, u32[]{:S(2)}, u32[]{:S(2)}) collective-permute-start(f32[5,8,8,128]{3,2,1,0:T(8,128)S(1)} %pad_maximum_fusion.3), channel_id=1, source_target_pairs={{0,1},{1,2},{2,3},{3,4},{4,5},{5,6},{6,7},{7,8},{8,9},{9,10},{10,1... | collective-permute-start | bytes 491528 | tf_op jit(solution)/shard_map/ppermute | solution.py:638
  16.3 7.4 %collective-permute-start.2 = (f32[5,7,8,256]{3,2,1,0:T(8,128)S(1)}, f32[5,7,8,256]{3,2,1,0:T(8,128)S(1)}, u32[]{:S(2)}, u32[]{:S(2)}) collective-permute-start(f32[5,7,8,256]{3,2,1,0:T(8,128)S(1)} %get-tuple-element.24), channel_id=1, source_target_pairs={{0,64},{64,128},{128,192},{192,256},{256,320},{320,384},{384,448},... | collective-permute-start | bytes 860168 | tf_op jit(solution)/shard_map/ppermute | solution.py:638
  17.6 10.2 %collective-permute-start.3 = (f32[5,7,8,256]{3,2,1,0:T(8,128)S(1)}, f32[5,7,8,256]{3,2,1,0:T(8,128)S(1)}, u32[]{:S(2)}, u32[]{:S(2)}) collective-permute-start(f32[5,7,8,256]{3,2,1,0:T(8,128)S(1)} %get-tuple-element.25), channel_id=1, source_target_pairs={{64,0},{128,64},{192,128},{256,192},{320,256},{384,320},{448,384},... | collective-permute-start | bytes 860168 | tf_op jit(solution)/shard_map/ppermute | solution.py:638
  27.9 24.2 %copy-start.6 = (f32[2,16]{1,0:T(2,128)S(1)}, f32[2,16]{1,0:T(2,128)}, u32[]{:S(2)}) copy-start(f32[2,16]{1,0:T(2,128)} %moduli.1) | copy-start | bytes 388
  27.9 23.1 %collective-permute-start.4 = (f32[5,22,8,256]{3,2,1,0:T(8,128)S(1)}, f32[5,22,8,256]{3,2,1,0:T(8,128)S(1)}, u32[]{:S(2)}, u32[]{:S(2)}) collective-permute-start(f32[5,22,8,256]{3,2,1,0:T(8,128)S(1)} %pad_maximum_fusion.1), channel_id=1, source_target_pairs={{16,0},{32,16},{48,32},{17,1},{33,17},{49,33},{18,2},{34,18},{50,3... | collective-permute-start | bytes 2703368 | tf_op jit(solution)/shard_map/ppermute | solution.py:638
  29.2 22.6 %collective-permute-start.5 = (f32[5,22,8,256]{3,2,1,0:T(8,128)S(1)}, f32[5,22,8,256]{3,2,1,0:T(8,128)S(1)}, u32[]{:S(2)}, u32[]{:S(2)}) collective-permute-start(f32[5,22,8,256]{3,2,1,0:T(8,128)S(1)} %pad_maximum_fusion.1), channel_id=1, source_target_pairs={{0,16},{16,32},{32,48},{1,17},{17,33},{33,49},{2,18},{18,34},{34,5... | collective-permute-start | bytes 2703368 | tf_op jit(solution)/shard_map/ppermute | solution.py:638
  113.6 0.9 copy-start
  114.5 0.9 copy-start.2
  115.5 0.9 copy-start.4
  117.1 19.4 %all-to-all-start.1 = ((f32[16,2,16,128]{3,2,1,0:T(8,128)}), f32[16,2,16,128]{3,2,1,0:T(8,128)S(1)}, u32[]{:S(2)}, u32[]{:S(2)}) async-start(f32[16,2,16,128]{3,2,1,0:T(8,128)} %broadcast_in_dim.30), calls=%async_computation.1 | async-start | bytes 524288 | tf_op jit(solution)/shard_map/all_to_all | solution.py:656
  136.5 1.2 copy-start.1
  137.6 1.1 copy-start.3
  138.8 1.1 copy-start.5

commit v3 on v2

--- a/solution.py
+++ b/solution.py
@@ -10,7 +10,7 @@
 THETA = 1.125
 HALF = 0.875
 SIGMA = THETA / HALF
-VMEM_LIMIT = 28 * 1024 * 1024
+VMEM_LIMIT = 36 * 1024 * 1024
 
 
 def cheb_factors():
@@ -373,29 +373,99 @@
     return back + roll(back, 32, 1) + roll(back, 64, 1)
 
 
-def eliminate(mat, cells):
-    tiles = [jnp.stack([mat[c, k, 8 * t : 8 * t + 8] for c, k in cells]) for t in range(4)]
-    rows = iota(tiles[0].shape, 1)
-    for p in range(0, 32, 2):
-        at, q = divmod(p, 8)
-        row0, row1 = tiles[at][:, q : q + 1, :], tiles[at][:, q + 1 : q + 2, :]
-        a00, a01 = row0[:, :, p : p + 1], row0[:, :, p + 1 : p + 2]
-        a10, a11 = row1[:, :, p : p + 1], row1[:, :, p + 1 : p + 2]
-        scale = 1.0 / (a00 * a11 - a01 * a10)
-        new0 = (a11 * scale) * row0 - (a01 * scale) * row1
-        new1 = (a00 * scale) * row1 - (a10 * scale) * row0
-        for t in range(4):
-            a = tiles[t]
-            a = a - (a[:, :, p : p + 1] * new0 + a[:, :, p + 1 : p + 2] * new1)
-            if t == at:
-                a = jnp.where(rows == q, new0, jnp.where(rows == q + 1, new1, a))
-            tiles[t] = a
-    for n, (c, k) in enumerate(cells):
-        for t in range(4):
-            mat[c, k, 8 * t : 8 * t + 8] = tiles[t][n]
-
-
-def coarse_solve(mods3, rest, mat):
+def lane_of(v, p):
+    return jnp.broadcast_to(v[:, p : p + 1], v.shape)
+
+
+def eliminate(sources, targets, band, kept):
+    rows = [[get(i) for i in range(32)] for get in sources]
+    slot = {}
+    for p in range(0, 32, 4):
+        last = min(32, p + 4 + band)
+        for n, a in enumerate(rows):
+            r = a[p : p + 4]
+            b = [[lane_of(v, p + k) for k in range(4)] for v in r]
+            scale = 1.0 / (b[0][0] * b[1][1] - b[0][1] * b[1][0])
+            u00, u01, u10, u11 = b[1][1] * scale, b[0][1] * scale, b[1][0] * scale, b[0][0] * scale
+            h0 = [u00 * b[0][k] - u01 * b[1][k] for k in (2, 3)]
+            h1 = [u11 * b[1][k] - u10 * b[0][k] for k in (2, 3)]
+            c2 = [b[2][k + 2] - (b[2][0] * h0[k] + b[2][1] * h1[k]) for k in (0, 1)]
+            c3 = [b[3][k + 2] - (b[3][0] * h0[k] + b[3][1] * h1[k]) for k in (0, 1)]
+            scale = 1.0 / (c2[0] * c3[1] - c2[1] * c3[0])
+            w00, w01, w10, w11 = c3[1] * scale, c2[1] * scale, c3[0] * scale, c2[0] * scale
+
+            def solve(v):
+                n0, n1 = u00 * v[0] - u01 * v[1], u11 * v[1] - u10 * v[0]
+                v2 = v[2] - (b[2][0] * n0 + b[2][1] * n1)
+                v3 = v[3] - (b[3][0] * n0 + b[3][1] * n1)
+                n2, n3 = w00 * v2 - w01 * v3, w11 * v3 - w10 * v2
+                return [n0 - (h0[0] * n2 + h0[1] * n3), n1 - (h1[0] * n2 + h1[1] * n3), n2, n3]
+
+            new = solve(r)
+            for i in range(p + 4, last):
+                f = [lane_of(r[k], i) if i - p - k <= band else jnp.zeros((8, 128), F32) for k in range(4)]
+                a[i] = a[i] - ((f[0] * new[0] + f[1] * new[1]) + (f[2] * new[2] + f[3] * new[3]))
+                at = slot.setdefault((p, i), 4 * len(slot))
+                for k, v in enumerate(solve(f)):
+                    kept[n, at + k] = v
+            a[p : p + 4] = new
+    for p in range(24, -1, -4):
+        last = min(32, p + 4 + band)
+        for n, a in enumerate(rows):
+            for k in range(4):
+                x = a[p + k]
+                for i in range(last - 1, p + 3, -1):
+                    x = x - kept[n, slot[p, i] + k] * a[i]
+                a[p + k] = x
+    for a, put in zip(rows, targets):
+        for i in range(32):
+            put(i, a[i])
+
+
+def reader(ref, *at):
+    return lambda i: ref[at + (slice(8 * i, 8 * i + 8),)]
+
+
+def writer(ref, *at):
+    def put(i, v):
+        ref[at + (slice(8 * i, 8 * i + 8),)] = v
+
+    return put
+
+
+def one_system(n):
+    return pl.ds(n, 32, 8)
+
+
+def reduced(m, before, after):
+    lane = iota((32, 128), 1)
+    inner, outer = lane < 32, lane >= 96
+    none = jnp.zeros((32, 128), F32)
+    left, right = none, none
+    if before is not None:
+        left = jnp.where(inner, roll(before, 64, 1), jnp.where((lane < 64) | outer, before, 0.0))
+    if after is not None:
+        right = jnp.where(inner, roll(after, 96, 1), jnp.where(lane >= 64, after, 0.0))
+    high, low = split(roll(m, -32, 1))
+    both = jnp.where(lane < 64, high.astype(F32), roll(low.astype(F32), 64, 1)).astype(BF16)
+    w_high, w_low = split(jnp.concatenate([left, right], axis=0))
+    change = mxu(
+        jnp.concatenate([both, both], axis=1), jnp.concatenate([w_high, w_high, w_low, w_low], axis=0)
+    )
+    return jnp.where(inner | outer, m, 0.0) - change
+
+
+def substitute(get, before, after):
+    lane = iota((8, 128), 1)
+    v = jnp.where(lane < 96, jnp.where(lane < 64, -before, -after), 1.0)
+    v = jnp.where(lane < 32, 0.0, v)
+    x = jnp.zeros((8, 128), F32)
+    for i in range(32):
+        x = jnp.where(lane % 32 == i, jnp.sum(get(i) * v, axis=1, keepdims=True), x)
+    return x
+
+
+def coarse_solve(mods3, rest, rows16, odd, even, solved, low, kept):
     blocks = ones_where(iota((16, 256), 1) // 16 == iota((16, 256), 0))
     shear = 0.0625 * dot_l(blocks, mods3[0])
     lame = 0.0625 * dot_l(blocks, mods3[1])
@@ -408,14 +478,10 @@
     for face, (axis, shift, below, above) in zip(faces, steps):
         uppers.append(jnp.where(above, roll(face, -shift, axis), 0.0))
     lane16 = iota((16, 128), 1)
-    row = iota((32, 128), 0)
-    lane = iota((32, 128), 1)
-    at_diag = lane % 32 == row
-    inner = lane < 32
-    patterns = (inner & (lane == row - 4), inner & (lane == row + 4), inner & (lane == row - 1), inner & (lane == row + 1))
-    columns = jnp.concatenate([faces[2], uppers[2]] + [jnp.zeros((16, 128), F32)] * 6, axis=0).T
-    for c in range(3):
-        first = jnp.where(
+    lane = iota((8, 128), 1)
+    sub = iota((8, 128), 0)
+    for c in range(3):
+        rows16[c, 0] = jnp.where(
             lane16 < 32,
             roll(diag, -32 * c, 1),
             jnp.where(
@@ -424,71 +490,66 @@
                 jnp.where(lane16 < 96, -roll(uppers[2], 64 - 32 * c, 1), roll(side, 96 - 32 * c, 1)),
             ),
         )
-        others = [-roll(v, -32 * c, 1) for v in (uppers[0], faces[0], uppers[1], faces[1])]
-        for k in range(16):
-            m = jnp.where(at_diag, first[k : k + 1], 0.0)
-            for pattern, v in zip(patterns, others):
-                m = jnp.where(pattern, v[k : k + 1], m)
-            mat[c, k] = m
-
-    lane_t = inner
-    lane_l = (lane >= 32) & (lane < 64)
-    lane_r = (lane >= 64) & (lane < 96)
-    lane_b = lane >= 96
-    keep = lane_t | lane_b
-    none = jnp.zeros((32, 128), F32)
-    for h in (1, 2, 4, 8):
-        eliminate(mat, [(c, k) for c in range(3) for k in range(h, 16, 2 * h)])
-        for c in range(3):
-            for k in range(0, 16, 2 * h):
-                m = mat[c, k]
-                left, right = none, none
-                if k - h >= 0:
-                    w = mat[c, k - h]
-                    left = jnp.where(lane_t, roll(w, 64, 1), jnp.where(lane_l | lane_b, w, 0.0))
-                if k + h < 16:
-                    w = mat[c, k + h]
-                    right = jnp.where(lane_t, roll(w, 96, 1), jnp.where(lane_r | lane_b, w, 0.0))
-                if h == 1:
-                    part = columns[32 * c : 32 * c + 32]
-                    change = -(part[:, k : k + 1] * left + part[:, 16 + k : 17 + k] * right)
-                else:
-                    high, low = split(roll(m, -32, 1))
-                    both = jnp.where(lane < 64, high.astype(F32), roll(low.astype(F32), 64, 1)).astype(BF16)
-                    w_high, w_low = split(jnp.concatenate([left, right], axis=0))
-                    change = mxu(
-                        jnp.concatenate([both, both], axis=1),
-                        jnp.concatenate([w_high, w_high, w_low, w_low], axis=0),
-                    )
-                mat[c, k] = jnp.where(keep, m, 0.0) - change
-    eliminate(mat, [(c, 0) for c in range(3)])
-    pieces = []
-    found = {}
-    for c in range(3):
-        found[c, 0] = jnp.sum(jnp.where(lane_b, mat[c, 0], 0.0), axis=1, keepdims=True)
-    for h in (8, 4, 2, 1):
-        for c in range(3):
-            for k in range(h, 16, 2 * h):
-                v = jnp.where(lane_l & at_diag, -found[c, k - h], 0.0)
-                if k + h < 16:
-                    v = jnp.where(lane_r & at_diag, -found[c, k + h], v)
-                v = jnp.sum(v, axis=0, keepdims=True)
-                v = jnp.where(lane_b[0:1], 1.0, v)
-                found[c, k] = jnp.sum(mat[c, k] * v, axis=1, keepdims=True)
-    for c in range(3):
-        piece = none
-        for k in range(16):
-            piece = jnp.where(lane == k, found[c, k], piece)
-        pieces.append(piece)
-    pieces.append(none)
-    whole = jnp.concatenate(pieces, axis=0)
-    again = ones_where(iota((256, 128), 0) // 16 == iota((256, 128), 1))
-    return dot_l_nt(again, whole)
+        for q, v in enumerate((uppers[0], faces[0], uppers[1], faces[1])):
+            rows16[c, q + 1] = -roll(v, -32 * c, 1)
+    for c in range(3):
+        for start, ref in ((0, even), (1, odd)):
+            first, x_up, x_down, y_up, y_down = [rows16.at[c, q][pl.ds(start, 8, 2)] for q in range(5)]
+            for i in range(32):
+                m = jnp.where(lane % 32 == i, first, 0.0)
+                for j, v in ((i - 4, x_up), (i + 4, x_down), (i - 1, y_up), (i + 1, y_down)):
+                    if 0 <= j < 32:
+                        m = jnp.where(lane == j, v, m)
+                ref[c, 8 * i : 8 * i + 8] = m
+    eliminate([reader(odd, c) for c in range(3)], [writer(odd, c) for c in range(3)], 4, kept)
+    inner, outer = lane < 32, lane >= 96
+    for c in range(3):
+        for i in range(32):
+            m = even[c, 8 * i : 8 * i + 8]
+            w = odd[c, 8 * i : 8 * i + 8]
+            before = roll(w, 1, 0)
+            left = jnp.where(inner, roll(before, 64, 1), jnp.where((lane < 64) | outer, before, 0.0))
+            right = jnp.where(inner, roll(w, 96, 1), jnp.where(lane >= 64, w, 0.0))
+            change = lane_of(m, 32 + i) * left + lane_of(m, 64 + i) * right
+            even[c, 8 * i : 8 * i + 8] = jnp.where(inner | outer, m, 0.0) - change
+    eliminate([reader(even, c) for c in range(3)], [writer(solved, c) for c in range(3)], 32, kept)
+    for c in range(3):
+        for n, (to, at) in {0: (1, c), 2: (0, c), 4: (1, 3 + c), 6: (0, 3 + c)}.items():
+            before = solved.at[c][one_system(n - 1)] if n > 0 else None
+            low.at[to][one_system(at)] = reduced(even.at[c][one_system(n)], before, solved.at[c][one_system(n + 1)])
+    eliminate([reader(low, 0)], [writer(low, 0)], 32, kept)
+    for c in range(3):
+        w4, w12 = low.at[0][one_system(c)], low.at[0][one_system(3 + c)]
+        low.at[3][one_system(c)] = reduced(low.at[1][one_system(c)], None, w4)
+        low.at[2][one_system(c)] = reduced(low.at[1][one_system(3 + c)], w4, w12)
+    eliminate([reader(low, 2)], [writer(low, 2)], 32, kept)
+    for c in range(3):
+        low.at[4][one_system(c)] = reduced(low.at[3][one_system(c)], None, low.at[2][one_system(c)])
+    eliminate([reader(low, 4)], [writer(low, 4)], 32, kept)
+    zero = jnp.zeros((8, 128), F32)
+    x0 = substitute(reader(low, 4), zero, zero)
+    x8 = substitute(reader(low, 2), x0, zero)
+    x4 = substitute(reader(low, 0), jnp.where(sub < 3, x0, roll(x8, 3, 0)), jnp.where(sub < 3, x8, 0.0))
+    group16 = iota((8, 128), 1) // 32
+    all_even, all_odd = zero, zero
+    for c in range(3):
+        x = zero
+        for n, v in ((0, x0[c : c + 1]), (2, x4[c : c + 1]), (4, x8[c : c + 1]), (6, x4[3 + c : 4 + c])):
+            x = jnp.where(sub == n, v, x)
+        after = jnp.where(sub < 7, roll(x, -1, 0), 0.0)
+        x = jnp.where(sub % 2 == 1, substitute(reader(solved, c), roll(x, 1, 0), after), x)
+        after = jnp.where(sub < 7, roll(x, -1, 0), 0.0)
+        all_even = jnp.where(group16 == c, x, all_even)
+        all_odd = jnp.where(group16 == c, substitute(reader(odd, c), x, after), all_odd)
+    plane = iota((256, 16), 0) // 16
+    place = iota((256, 16), 1)
+    place = jnp.where(place < 8, 2 * place, 2 * place - 15)
+    return dot_l(ones_where(plane == place), jnp.concatenate([all_even, all_odd], axis=0))
 
 
 def kernel_c(
     place, got, mod1, x1, r1, mod2, x2, r2, mod0, x0, r0, disp, resid,
-    mat, e3, e1, faces1, diag1, inv1, d1a, d1b, r1w, faces, diag, inv, d_a, d_b, r_w,
+    rows16, odd, even, solved, low, kept, e3, e1, faces1, diag1, inv1, d1a, d1b, r1w, faces, diag, inv, d_a, d_b, r_w,
 ):
     gx, gy, gz = place[0], place[1], place[2]
     b3 = jnp.concatenate([got[k, 0] for k in range(16)], axis=0)
@@ -497,7 +558,7 @@
     steps = level3_steps(256)
     factors = flat_factors(mods3, steps, (8.0, 8.0, 8.0), level3_groups(256))
     x, r = flat_smooth(None, b3, factors, steps, True)
-    corr = coarse_solve(mods3, r, mat)
+    corr = coarse_solve(mods3, r, rows16, odd, even, solved, low, kept)
     x = x + corr
     r = r - flat_apply(corr, factors, steps)
     x, _ = flat_smooth(x, r, factors, steps, False)
@@ -624,7 +685,8 @@
         out_shape=(shaped(3, 8, 8, 128), shaped(3, 8, 8, 128)),
         in_specs=[IN_SMEM] + [IN_VMEM] * 10,
         out_specs=(IN_VMEM,) * 2,
-        scratch_shapes=[scratch(3, 16, 32, 128), scratch(272, 128), scratch(*one)]
+        scratch_shapes=[scratch(3, 5, 16, 128)] + [scratch(3, 256, 128)] * 3
+        + [scratch(5, 256, 128), scratch(3, 448, 8, 128), scratch(272, 128), scratch(*one)]
         + [scratch(6, 34, 16, 128)] + [scratch(*one)] * 5
         + [scratch(6, 22, 24, 256)] + [scratch(*zero)] * 5,
         **PARAMS,

time: 190 us -> 169 us (0.89)
  Pallas kernels: 65.9 us -> 44.5 us
    pallas_call x1, Pallas kernels: 49.9 us -> 28.5 us  [call_c(): pl.pallas_call(kernel_c, out_shape=(shaped(3, 8, 8, 128), shaped(3, 8, 8,...]
where the time goes in v3:
time: 169 us; the launch traced here: 168 us
  blocking collectives  45.4 us (27%)
  Pallas kernels  44.5 us (26%)
  waiting for transfers between devices  41.3 us (24%)
  starting transfers between devices  26.3 us (16%)
  local copies, waits for them, and re-layouts  7.11 us (4%)
  other arithmetic  3.03 us (2%)
    all_to_all x1, blocking collectives, to_all(): return lax.all_to_all(copies, axes, 0, 0, tiled=True)  45.4 us
    pallas_call x1, Pallas kernels, call_c(): pl.pallas_call(kernel_c, out_shape=(shaped(3, 8, 8, 128), shaped(3, 8, 8,...  28.5 us
    ppermute x3, waiting for transfers between devices, both_ways(): lax.ppermute(to_before, axis, down)  21.9 us
    all_to_all x1, waiting for transfers between devices, to_all(): return lax.all_to_all(copies, axes, 0, 0, tiled=True)  11.6 us
    ppermute x3, starting transfers between devices, both_ways(): lax.ppermute(to_before, axis, down)  11.4 us
    pallas_call x1, Pallas kernels, call_b(): pl.pallas_call(kernel_b, out_shape=(shaped(2, 16, 128),) + (shaped(*one),...  8.54 us
    ppermute x3, waiting for transfers between devices, both_ways(): lax.ppermute(to_next, axis, up)  7.84 us
    all_to_all x1, starting transfers between devices, to_all(): return lax.all_to_all(copies, axes, 0, 0, tiled=True)  7.66 us
  transfers between devices with their start and end apart: 7, of which 6 were waited for; matrix products, arithmetic and copies ran while one was open for 0% of the time, Pallas kernels for 0%

profile of v3, /device:TPU:1, one launch (start us, length us, event | category | flops | bytes accessed | tf_op | source)
XLA Modules:
  0.0 168.4 jit_solution(10844042260607081557)
XLA Ops:
  0.6 0.0 copy-start.7
  0.6 0.8 convert_bitcast_fusion
  1.5 0.9 pad_maximum_fusion.3
  2.4 8.8 %collective-permute-start = (f32[5,8,8,128]{3,2,1,0:T(8,128)S(1)}, f32[5,8,8,128]{3,2,1,0:T(8,128)S(1)}, u32[]{:S(2)}, u32[]{:S(2)}) collective-permute-start(f32[5,8,8,128]{3,2,1,0:T(8,128)S(1)} %pad_maximum_fusion.3), channel_id=1, source_target_pairs={{1,0},{2,1},{3,2},{4,3},{5,4},{6,5},{7,6},{8,7},{9,8},{10,9},{11,1... | collective-permute-start | bytes 491528 | tf_op jit(solution)/shard_map/ppermute | solution.py:700
  11.2 1.9 %collective-permute-start.1 = (f32[5,8,8,128]{3,2,1,0:T(8,128)S(1)}, f32[5,8,8,128]{3,2,1,0:T(8,128)S(1)}, u32[]{:S(2)}, u32[]{:S(2)}) collective-permute-start(f32[5,8,8,128]{3,2,1,0:T(8,128)S(1)} %pad_maximum_fusion.3), channel_id=1, source_target_pairs={{0,1},{1,2},{2,3},{3,4},{4,5},{5,6},{6,7},{7,8},{8,9},{9,10},{10,1... | collective-permute-start | bytes 491528 | tf_op jit(solution)/shard_map/ppermute | solution.py:700
  13.1 0.0 collective-permute-done
  13.1 2.2 %collective-permute-done.1 = f32[5,8,8,128]{3,2,1,0:T(8,128)S(1)} collective-permute-done((f32[5,8,8,128]{3,2,1,0:T(8,128)S(1)}, f32[5,8,8,128]{3,2,1,0:T(8,128)S(1)}, u32[]{:S(2)}, u32[]{:S(2)}) %collective-permute-start.1) | collective-permute-done | bytes 163872 | tf_op jit(solution)/shard_map/ppermute | solution.py:700
  15.4 0.9 pad_maximum_fusion.2
  16.3 1.3 collective-permute-start.2
  17.6 1.3 collective-permute-start.3
  18.9 4.8 %collective-permute-done.2 = f32[5,7,8,256]{3,2,1,0:T(8,128)S(1)} collective-permute-done((f32[5,7,8,256]{3,2,1,0:T(8,128)S(1)}, f32[5,7,8,256]{3,2,1,0:T(8,128)S(1)}, u32[]{:S(2)}, u32[]{:S(2)}) %collective-permute-start.2) | collective-permute-done | bytes 286752 | tf_op jit(solution)/shard_map/ppermute | solution.py:700
  23.7 4.1 %collective-permute-done.3 = f32[5,7,8,256]{3,2,1,0:T(8,128)S(1)} collective-permute-done((f32[5,7,8,256]{3,2,1,0:T(8,128)S(1)}, f32[5,7,8,256]{3,2,1,0:T(8,128)S(1)}, u32[]{:S(2)}, u32[]{:S(2)}) %collective-permute-start.3) | collective-permute-done | bytes 286752 | tf_op jit(solution)/shard_map/ppermute | solution.py:700
  27.8 0.0 copy-done.7
  27.8 0.1 pad_maximum_fusion.1
  27.9 0.0 copy-start.6
  27.9 1.3 collective-permute-start.4
  29.2 4.0 %collective-permute-start.5 = (f32[5,22,8,256]{3,2,1,0:T(8,128)S(1)}, f32[5,22,8,256]{3,2,1,0:T(8,128)S(1)}, u32[]{:S(2)}, u32[]{:S(2)}) collective-permute-start(f32[5,22,8,256]{3,2,1,0:T(8,128)S(1)} %pad_maximum_fusion.1), channel_id=1, source_target_pairs={{0,16},{16,32},{32,48},{1,17},{17,33},{33,49},{2,18},{18,34},{34,5... | collective-permute-start | bytes 2703368 | tf_op jit(solution)/shard_map/ppermute | solution.py:700
  33.3 17.7 %collective-permute-done.4 = f32[5,22,8,256]{3,2,1,0:T(8,128)S(1)} collective-permute-done((f32[5,22,8,256]{3,2,1,0:T(8,128)S(1)}, f32[5,22,8,256]{3,2,1,0:T(8,128)S(1)}, u32[]{:S(2)}, u32[]{:S(2)}) %collective-permute-start.4) | collective-permute-done | bytes 901152 | tf_op jit(solution)/shard_map/ppermute | solution.py:700
  51.0 0.9 collective-permute-done.5
  51.9 0.2 pad_maximum_fusion.ext
  52.1 0.0 copy-done.6
  52.1 7.5 %shard_map.59 = (f32[80,128]{1,0:T(8,128)S(1)}, f32[3,14,24,256]{3,2,1,0:T(8,128)S(1)}, f32[3,8,8,128]{3,2,1,0:T(8,128)S(1)}, f32[3,22,24,256]{3,2,1,0:T(8,128)S(1)}) custom-call(f32[2,16]{1,0:T(2,128)S(1)} %copy-done.6, f32[5,22,24,256]{3,2,1,0:T(8,128)S(1)} %pad_maximum_fusion.ext), custom_call_target="tpu_custom_call" | custom-call | tf_op jit(solution)/shard_map/pallas_call | solution.py:659
  59.6 0.1 broadcast_in_dim.29
  59.7 45.4 %all_to_all.10.got = f32[32,80,128]{2,1,0:T(8,128)S(1)} all-to-all(f32[32,80,128]{2,1,0:T(8,128)S(1)} %broadcast_in_dim.29), channel_id=1, replica_groups=mesh['gx'=8,'gy'=4,'gz'=16] {'gx','gy'}, dimensions={0} | all-to-all | bytes 2621440 | tf_op jit(solution)/shard_map/all_to_all | solution.py:718
  105.0 8.5 %shard_map.60 = (f32[2,16,128]{2,1,0:T(8,128)S(1)}, f32[3,34,16,128]{3,2,1,0:T(8,128)S(1)}, f32[3,34,16,128]{3,2,1,0:T(8,128)S(1)}, f32[3,34,16,128]{3,2,1,0:T(8...) custom-call(f32[32,80,128]{2,1,0:T(8,128)S(1)} %all_to_all.10.got), custom_call_target="tpu_custom_call" | custom-call | tf_op jit(solution)/shard_map/pallas_call | solution.py:671
  113.6 0.0 copy-start
  113.6 0.9 copy-done
  114.5 0.0 copy-start.2
  114.5 0.9 copy-done.2
  115.4 0.0 copy-start.4
  115.5 0.9 copy-done.4
  116.4 0.7 broadcast_in_dim.30
  117.1 7.7 %all-to-all-start.1 = ((f32[16,2,16,128]{3,2,1,0:T(8,128)}), f32[16,2,16,128]{3,2,1,0:T(8,128)S(1)}, u32[]{:S(2)}, u32[]{:S(2)}) async-start(f32[16,2,16,128]{3,2,1,0:T(8,128)} %broadcast_in_dim.30), calls=%async_computation.1 | async-start | bytes 524288 | tf_op jit(solution)/shard_map/all_to_all | solution.py:718
  124.8 0.1 pad_add_fusion.place
  124.8 11.6 %all-to-all-done.1.got = f32[16,2,16,128]{3,2,1,0:T(8,128)S(1)} async-done(((f32[16,2,16,128]{3,2,1,0:T(8,128)}), f32[16,2,16,128]{3,2,1,0:T(8,128)S(1)}, u32[]{:S(2)}, u32[]{:S(2)}) %all-to-all-start.1) | async-done | bytes 262176 | tf_op jit(solution)/shard_map/all_to_all | solution.py:718
  136.5 0.0 copy-start.1
  136.5 1.1 copy-done.1
  137.6 0.0 copy-start.3
  137.6 1.1 copy-done.3
  138.8 0.0 copy-start.5
  138.8 1.1 copy-done.5
  139.9 28.5 %shard_map.61 = (f32[3,8,8,128]{3,2,1,0:T(8,128)}, f32[3,8,8,128]{3,2,1,0:T(8,128)}) custom-call(s32[3]{0:T(128)S(1)} %pad_add_fusion.place, f32[16,2,16,128]{3,2,1,0:T(8,128)S(1)} %all-to-all-done.1.got, f32[3,34,16,128]{3,2,1,0:T(8,128)S(1)} %copy-done.1, f32[3,34,16,128]{3,2,1,0:T(8,128)S(1)} %copy-done.3, f32[3,34,16,128]{3,2,1,0:T(8,128)S(1)} %copy-done.5, ...), custom_call_target="tpu_custom_call" | custom-call | tf_op jit(solution)/shard_map/pallas_call | solution.py:683
  (3 shorter events, 0.1 us)
Async XLA Ops:
  0.6 27.2 %copy-start.7 = (f32[3,8,8,128]{3,2,1,0:T(8,128)S(1)}, f32[3,8,8,128]{3,2,1,0:T(8,128)}, u32[]{:S(2)}) copy-start(f32[3,8,8,128]{3,2,1,0:T(8,128)} %param.4) | copy-start | bytes 294916
  2.4 10.7 %collective-permute-start = (f32[5,8,8,128]{3,2,1,0:T(8,128)S(1)}, f32[5,8,8,128]{3,2,1,0:T(8,128)S(1)}, u32[]{:S(2)}, u32[]{:S(2)}) collective-permute-start(f32[5,8,8,128]{3,2,1,0:T(8,128)S(1)} %pad_maximum_fusion.3), channel_id=1, source_target_pairs={{1,0},{2,1},{3,2},{4,3},{5,4},{6,5},{7,6},{8,7},{9,8},{10,9},{11,1... | collective-permute-start | bytes 491528 | tf_op jit(solution)/shard_map/ppermute | solution.py:700
  11.2 4.2 %collective-permute-start.1 = (f32[5,8,8,128]{3,2,1,0:T(8,128)S(1)}, f32[5,8,8,128]{3,2,1,0:T(8,128)S(1)}, u32[]{:S(2)}, u32[]{:S(2)}) collective-permute-start(f32[5,8,8,128]{3,2,1,0:T(8,128)S(1)} %pad_maximum_fusion.3), channel_id=1, source_target_pairs={{0,1},{1,2},{2,3},{3,4},{4,5},{5,6},{6,7},{7,8},{8,9},{9,10},{10,1... | collective-permute-start | bytes 491528 | tf_op jit(solution)/shard_map/ppermute | solution.py:700
  16.3 7.4 %collective-permute-start.2 = (f32[5,7,8,256]{3,2,1,0:T(8,128)S(1)}, f32[5,7,8,256]{3,2,1,0:T(8,128)S(1)}, u32[]{:S(2)}, u32[]{:S(2)}) collective-permute-start(f32[5,7,8,256]{3,2,1,0:T(8,128)S(1)} %get-tuple-element.24), channel_id=1, source_target_pairs={{0,64},{64,128},{128,192},{192,256},{256,320},{320,384},{384,448},... | collective-permute-start | bytes 860168 | tf_op jit(solution)/shard_map/ppermute | solution.py:700
  17.6 10.2 %collective-permute-start.3 = (f32[5,7,8,256]{3,2,1,0:T(8,128)S(1)}, f32[5,7,8,256]{3,2,1,0:T(8,128)S(1)}, u32[]{:S(2)}, u32[]{:S(2)}) collective-permute-start(f32[5,7,8,256]{3,2,1,0:T(8,128)S(1)} %get-tuple-element.25), channel_id=1, source_target_pairs={{64,0},{128,64},{192,128},{256,192},{320,256},{384,320},{448,384},... | collective-permute-start | bytes 860168 | tf_op jit(solution)/shard_map/ppermute | solution.py:700
  27.9 24.2 %copy-start.6 = (f32[2,16]{1,0:T(2,128)S(1)}, f32[2,16]{1,0:T(2,128)}, u32[]{:S(2)}) copy-start(f32[2,16]{1,0:T(2,128)} %moduli.1) | copy-start | bytes 388
  27.9 23.1 %collective-permute-start.4 = (f32[5,22,8,256]{3,2,1,0:T(8,128)S(1)}, f32[5,22,8,256]{3,2,1,0:T(8,128)S(1)}, u32[]{:S(2)}, u32[]{:S(2)}) collective-permute-start(f32[5,22,8,256]{3,2,1,0:T(8,128)S(1)} %pad_maximum_fusion.1), channel_id=1, source_target_pairs={{16,0},{32,16},{48,32},{17,1},{33,17},{49,33},{18,2},{34,18},{50,3... | collective-permute-start | bytes 2703368 | tf_op jit(solution)/shard_map/ppermute | solution.py:700
  29.2 22.6 %collective-permute-start.5 = (f32[5,22,8,256]{3,2,1,0:T(8,128)S(1)}, f32[5,22,8,256]{3,2,1,0:T(8,128)S(1)}, u32[]{:S(2)}, u32[]{:S(2)}) collective-permute-start(f32[5,22,8,256]{3,2,1,0:T(8,128)S(1)} %pad_maximum_fusion.1), channel_id=1, source_target_pairs={{0,16},{16,32},{32,48},{1,17},{17,33},{33,49},{2,18},{18,34},{34,5... | collective-permute-start | bytes 2703368 | tf_op jit(solution)/shard_map/ppermute | solution.py:700
  113.6 0.9 copy-start
  114.5 0.9 copy-start.2
  115.4 0.9 copy-start.4
  117.1 19.4 %all-to-all-start.1 = ((f32[16,2,16,128]{3,2,1,0:T(8,128)}), f32[16,2,16,128]{3,2,1,0:T(8,128)S(1)}, u32[]{:S(2)}, u32[]{:S(2)}) async-start(f32[16,2,16,128]{3,2,1,0:T(8,128)} %broadcast_in_dim.30), calls=%async_computation.1 | async-start | bytes 524288 | tf_op jit(solution)/shard_map/all_to_all | solution.py:718
  136.5 1.2 copy-start.1
  137.6 1.1 copy-start.3
  138.8 1.1 copy-start.5

commit v4 on v3

--- a/solution.py
+++ b/solution.py
@@ -166,28 +166,32 @@
         mod[1, i] = lame
         mod[2, i] = ext[4, i]
 
-    loop(0, 22, look_up)
-    plane_factors(mod, 1.0, faces, diag, inv, 1, 21, False)
+    loop(0, 16, look_up)
+    for k in range(3):
+        mod[k, 16] = jnp.zeros((16, 256), F32)
+    plane_factors(mod, 1.0, faces, diag, inv, 1, 15, False)
 
     def start(i):
         for c in range(3):
             d_a[c, i] = (START[1] * inv[c, i]) * ext[c, i]
 
-    loop(1, 21, start)
-    plane_sweep(d_a, d_b, ext, r, faces, diag, inv, 2, 20, CHEB[0])
-    for c in range(3):
-        x_out[c] = d_a[c, 7:15, 0:8, 0:128] + d_b[c, 7:15, 0:8, 0:128]
-    plane_sweep(d_b, d_a, r, r, faces, diag, inv, 3, 19, CHEB[1])
-    for c in range(3):
-        x_out[c] = x_out[c] + d_a[c, 7:15, 0:8, 0:128]
-    plane_sweep(d_a, None, r, r_out, faces, diag, inv, 4, 18, None, 0, 4)
+    loop(1, 15, start)
+    plane_sweep(d_a, d_b, ext, r, faces, diag, inv, 2, 14, CHEB[0])
+    for c in range(3):
+        x_out[c] = d_a[c, 4:12, 0:8, 0:128] + d_b[c, 4:12, 0:8, 0:128]
+    plane_sweep(d_b, d_a, r, r, faces, diag, inv, 3, 13, CHEB[1])
+    for c in range(3):
+        x_out[c] = x_out[c] + d_a[c, 4:12, 0:8, 0:128]
+    plane_sweep(d_a, None, r, r, faces, diag, inv, 4, 12, None)
+    for c in range(3):
+        r_out[c] = r[c, 4:12, 0:8]
     rows = []
     for c in range(3):
         for j in range(4):
-            rows.append(r_out[c, 3 + 2 * j, 0:8] + r_out[c, 4 + 2 * j, 0:8])
+            rows.append(r_out[c, 2 * j] + r_out[c, 2 * j + 1])
     for k in range(3):
         for j in range(4):
-            rows.append(mod[k, 7 + 2 * j, 0:8] + mod[k, 8 + 2 * j, 0:8])
+            rows.append(mod[k, 4 + 2 * j, 0:8] + mod[k, 5 + 2 * j, 0:8])
     stacked = jnp.concatenate(rows, axis=0)
     pair_z = ones_where(iota((256, 128), 0) // 2 == iota((256, 128), 1))
     pair_y = ones_where(iota((96, 192), 1) // 2 == iota((96, 192), 0))
@@ -605,9 +609,9 @@
     plane_sweep(d1b, d1a, r1w, None, faces1, diag1, inv1, 1, 33, CHEB[1])
     for c in range(3):
         e1[c, 1:33] = e1[c, 1:33] + d1a[c, 1:33]
-    row = iota((24, 16), 0)
-    row = jnp.where(row >= 16, row - 24, row)
-    up_y = ones_where((row + 8 * gy + 16) // 2 - 8 == iota((24, 16), 1))
+    row = iota((16, 16), 0)
+    row = jnp.where(row >= 12, row - 16, row)
+    up_y = ones_where((row + 8 * gy + 16) // 2 - 8 == iota((16, 16), 1))
     up_z0 = ones_where(iota((128, 256), 1) // 2 == iota((128, 256), 0))
     planes = []
     for c in range(3):
@@ -620,22 +624,22 @@
             at = 16 * (8 * c + j)
             high, low = split(lifted[at : at + 16])
             plane = mxu(up_y, jnp.concatenate([high, low], axis=0))
-            d_b[c, 3 + 2 * j] = plane
-            d_b[c, 4 + 2 * j] = plane
-    plane_factors(mod0, 1.0, faces, diag, inv, 4, 19, False)
-    own_part = (slice(7, 15), slice(0, 8), slice(0, 128))
+            d_b[c, 2 * j] = plane
+            d_b[c, 2 * j + 1] = plane
+    plane_factors(mod0, 1.0, faces, diag, inv, 1, 16, False)
+    own_part = (slice(4, 12), slice(0, 8), slice(0, 128))
     for c in range(3):
         disp[c] = x0[c] + d_b[(c,) + own_part]
-    plane_sweep(d_b, d_a, r0, r_w, faces, diag, inv, 4, 18, START, 4, 0)
+    plane_sweep(d_b, d_a, r0, r_w, faces, diag, inv, 1, 15, START, 1, 0)
     for c in range(3):
         disp[c] = disp[c] + d_a[(c,) + own_part]
-    plane_sweep(d_a, d_b, r_w, r_w, faces, diag, inv, 5, 17, CHEB[0])
+    plane_sweep(d_a, d_b, r_w, r_w, faces, diag, inv, 2, 14, CHEB[0])
     for c in range(3):
         disp[c] = disp[c] + d_b[(c,) + own_part]
-    plane_sweep(d_b, d_a, r_w, r_w, faces, diag, inv, 6, 16, CHEB[1])
+    plane_sweep(d_b, d_a, r_w, r_w, faces, diag, inv, 3, 13, CHEB[1])
     for c in range(3):
         disp[c] = disp[c] + d_a[(c,) + own_part]
-    plane_sweep(d_a, None, r_w, r_w, faces, diag, inv, 7, 15, None)
+    plane_sweep(d_a, None, r_w, r_w, faces, diag, inv, 4, 12, None)
     for c in range(3):
         resid[c] = r_w[(c,) + own_part]
 
@@ -658,10 +662,10 @@
 def call_a(moduli, ext):
     return pl.pallas_call(
         kernel_a,
-        out_shape=(shaped(80, 128), shaped(3, 14, 24, 256), shaped(3, 8, 8, 128), shaped(3, 22, 24, 256)),
+        out_shape=(shaped(80, 128), shaped(3, 8, 8, 256), shaped(3, 8, 8, 128), shaped(3, 17, 16, 256)),
         in_specs=[IN_SMEM, IN_VMEM],
         out_specs=(IN_VMEM,) * 4,
-        scratch_shapes=[scratch(6, 22, 24, 256)] + [scratch(3, 22, 24, 256)] * 5,
+        scratch_shapes=[scratch(6, 17, 16, 256)] + [scratch(3, 17, 16, 256)] * 5,
         **PARAMS,
     )(moduli, ext)
 
@@ -679,7 +683,7 @@
 
 
 def call_c(place, got, level1, level2, level0):
-    one, zero = (3, 34, 16, 128), (3, 22, 24, 256)
+    one, zero = (3, 34, 16, 128), (3, 17, 16, 256)
     return pl.pallas_call(
         kernel_c,
         out_shape=(shaped(3, 8, 8, 128), shaped(3, 8, 8, 128)),
@@ -688,7 +692,7 @@
         scratch_shapes=[scratch(3, 5, 16, 128)] + [scratch(3, 256, 128)] * 3
         + [scratch(5, 256, 128), scratch(3, 448, 8, 128), scratch(272, 128), scratch(*one)]
         + [scratch(6, 34, 16, 128)] + [scratch(*one)] * 5
-        + [scratch(6, 22, 24, 256)] + [scratch(*zero)] * 5,
+        + [scratch(6, 17, 16, 256)] + [scratch(*zero)] * 5,
         **PARAMS,
     )(place, got, *level1, *level2, *level0)
 
@@ -707,9 +711,13 @@
     before, after = both_ways(cells, cells, "gz")
     halo = jnp.where(iota((1, 1, 1, 128), 3) < 64, after, before)
     cells = jnp.concatenate([cells, halo], axis=3)
-    before, after = both_ways(cells[:, 1:8], cells[:, 0:7], "gx")
+    return wider(cells, 4)
+
+
+def wider(cells, planes):
+    before, after = both_ways(cells[:, 8 - planes : 8], cells[:, 0:planes], "gx")
     cells = jnp.concatenate([before, cells, after], axis=1)
-    before, after = both_ways(cells, cells, "gy")
+    before, after = both_ways(cells[:, :, 4:8], cells[:, :, 0:4], "gy")
     return jnp.concatenate([cells, after, before], axis=2)
 
 
@@ -724,7 +732,7 @@
     send, mod1, x1, r1, mod2, x2, r2 = call_b(to_all(send, ("gx", "gy"), 32))
     got = to_all(send, "gz", 16)
     place = jnp.stack([lax.axis_index("gx"), lax.axis_index("gy"), lax.axis_index("gz")]).astype(jnp.int32)
-    return call_c(place, got, (mod1, x1, r1), (mod2, x2, r2), (mod0, x0, r0))
+    return call_c(place, got, (mod1, x1, r1), (mod2, x2, r2), (mod0, x0, wider(r0, 3)))
 
 
 def solution(mesh):

time: 169 us -> 150 us (0.89)
  blocking collectives: 45.4 us -> 0 us
  starting transfers between devices: 26.3 us -> 47.7 us
  waiting for transfers between devices: 41.3 us -> 49.1 us
  Pallas kernels: 44.5 us -> 39.8 us
    all_to_all x1 -> x0, blocking collectives: 45.4 us -> none  [to_all(): return lax.all_to_all(copies, axes, 0, 0, tiled=True)]
    ppermute x3 -> x5, waiting for transfers between devices: 7.84 us -> 35.4 us  [both_ways(): lax.ppermute(to_next, axis, up)]
    all_to_all x1 -> x2, starting transfers between devices: 7.66 us -> 19.6 us  [to_all(): return lax.all_to_all(copies, axes, 0, 0, tiled=True)]
    all_to_all x1 -> x2, waiting for transfers between devices: 11.6 us -> 1.1 us  [to_all(): return lax.all_to_all(copies, axes, 0, 0, tiled=True)]
    ppermute x3 -> x5, waiting for transfers between devices: 21.9 us -> 12.6 us  [both_ways(): lax.ppermute(to_before, axis, down)]
    ppermute x3 -> x5, starting transfers between devices: 7.27 us -> 13.9 us  [both_ways(): lax.ppermute(to_next, axis, up)]
    pallas_call x1, Pallas kernels: 7.46 us -> 4.01 us  [call_a(): pl.pallas_call(kernel_a, out_shape=(shaped(80, 128), shaped(3, 8, 8, 256)...]
    ppermute x3 -> x5, starting transfers between devices: 11.4 us -> 14.1 us  [both_ways(): lax.ppermute(to_before, axis, down)]
  transfers between devices with their start and end apart: 7 -> 12, of which waited for: 6 -> 10; matrix products, arithmetic and copies ran while one was open for 0% -> 2% of each run, Pallas kernels for 0% -> 0%
where the time goes in v4:
time: 150 us
  waiting for transfers between devices  49.1 us (33%)
  starting transfers between devices  47.7 us (32%)
  Pallas kernels  39.8 us (27%)
  local copies, waits for them, and re-layouts  8.12 us (5%)
  other arithmetic  3.98 us (3%)
    ppermute x5, waiting for transfers between devices, both_ways(): lax.ppermute(to_next, axis, up)  35.4 us
    pallas_call x1, Pallas kernels, call_c(): pl.pallas_call(kernel_c, out_shape=(shaped(3, 8, 8, 128), shaped(3, 8, 8,...  27.3 us
    all_to_all x2, starting transfers between devices, to_all(): return lax.all_to_all(copies, axes, 0, 0, tiled=True)  19.6 us
    ppermute x5, starting transfers between devices, both_ways(): lax.ppermute(to_before, axis, down)  14.1 us
    ppermute x5, starting transfers between devices, both_ways(): lax.ppermute(to_next, axis, up)  13.9 us
    ppermute x5, waiting for transfers between devices, both_ways(): lax.ppermute(to_before, axis, down)  12.6 us
    pallas_call x1, Pallas kernels, call_b(): pl.pallas_call(kernel_b, out_shape=(shaped(2, 16, 128),) + (shaped(*one),...  8.54 us
    unnamed x18, local copies, waits for them, and re-layouts  4.94 us
  transfers between devices with their start and end apart: 12, of which 10 were waited for; matrix products, arithmetic and copies ran while one was open for 2% of the time, Pallas kernels for 0%

profile of v4, /device:TPU:1, one launch (start us, length us, event | category | flops | bytes accessed | tf_op | source)
XLA Modules:
  0.0 149.6 jit_solution(2207928663469725809)
XLA Ops:
  0.6 0.0 copy-start.7
  0.6 0.8 convert_bitcast_fusion
  1.5 0.9 pad_maximum_fusion.4
  2.4 8.8 %collective-permute-start = (f32[5,8,8,128]{3,2,1,0:T(8,128)S(1)}, f32[5,8,8,128]{3,2,1,0:T(8,128)S(1)}, u32[]{:S(2)}, u32[]{:S(2)}) collective-permute-start(f32[5,8,8,128]{3,2,1,0:T(8,128)S(1)} %pad_maximum_fusion.4), channel_id=1, source_target_pairs={{1,0},{2,1},{3,2},{4,3},{5,4},{6,5},{7,6},{8,7},{9,8},{10,9},{11,1... | collective-permute-start | bytes 491528 | tf_op jit(solution)/shard_map/ppermute | solution.py:704
  11.2 1.9 %collective-permute-start.1 = (f32[5,8,8,128]{3,2,1,0:T(8,128)S(1)}, f32[5,8,8,128]{3,2,1,0:T(8,128)S(1)}, u32[]{:S(2)}, u32[]{:S(2)}) collective-permute-start(f32[5,8,8,128]{3,2,1,0:T(8,128)S(1)} %pad_maximum_fusion.4), channel_id=1, source_target_pairs={{0,1},{1,2},{2,3},{3,4},{4,5},{5,6},{6,7},{7,8},{8,9},{9,10},{10,1... | collective-permute-start | bytes 491528 | tf_op jit(solution)/shard_map/ppermute | solution.py:704
  13.1 0.0 collective-permute-done
  13.1 2.2 %collective-permute-done.1 = f32[5,8,8,128]{3,2,1,0:T(8,128)S(1)} collective-permute-done((f32[5,8,8,128]{3,2,1,0:T(8,128)S(1)}, f32[5,8,8,128]{3,2,1,0:T(8,128)S(1)}, u32[]{:S(2)}, u32[]{:S(2)}) %collective-permute-start.1) | collective-permute-done | bytes 163872 | tf_op jit(solution)/shard_map/ppermute | solution.py:704
  15.4 0.9 pad_maximum_fusion.3
  16.3 1.3 collective-permute-start.3
  17.6 4.0 %collective-permute-start.2 = (f32[5,4,8,256]{3,2,1,0:T(8,128)S(1)}, f32[5,4,8,256]{3,2,1,0:T(8,128)S(1)}, u32[]{:S(2)}, u32[]{:S(2)}) collective-permute-start(f32[5,4,8,256]{3,2,1,0:T(8,128)S(1)} %get-tuple-element.28), channel_id=1, source_target_pairs={{0,64},{64,128},{128,192},{192,256},{256,320},{320,384},{384,448},... | collective-permute-start | bytes 491528 | tf_op jit(solution)/shard_map/ppermute | solution.py:704
  21.6 2.3 %collective-permute-done.3 = f32[5,4,8,256]{3,2,1,0:T(8,128)S(1)} collective-permute-done((f32[5,4,8,256]{3,2,1,0:T(8,128)S(1)}, f32[5,4,8,256]{3,2,1,0:T(8,128)S(1)}, u32[]{:S(2)}, u32[]{:S(2)}) %collective-permute-start.3) | collective-permute-done | bytes 163872 | tf_op jit(solution)/shard_map/ppermute | solution.py:704
  23.9 1.7 %collective-permute-done.2 = f32[5,4,8,256]{3,2,1,0:T(8,128)S(1)} collective-permute-done((f32[5,4,8,256]{3,2,1,0:T(8,128)S(1)}, f32[5,4,8,256]{3,2,1,0:T(8,128)S(1)}, u32[]{:S(2)}, u32[]{:S(2)}) %collective-permute-start.2) | collective-permute-done | bytes 163872 | tf_op jit(solution)/shard_map/ppermute | solution.py:704
  25.6 0.0 copy-done.7
  25.6 0.1 pad_maximum_fusion.2
  25.7 0.1 fusion
  25.8 1.3 collective-permute-start.5
  27.1 0.0 copy-start.4
  27.1 1.3 collective-permute-start.4
  28.4 5.7 %collective-permute-done.5 = f32[5,16,4,256]{3,2,1,0:T(4,128)S(1)} collective-permute-done((f32[5,16,4,256]{3,2,1,0:T(4,128)S(1)}, f32[5,16,4,256]{3,2,1,0:T(4,128)S(1)}, u32[]{:S(2)}, u32[]{:S(2)}) %collective-permute-start.5) | collective-permute-done | bytes 327712 | tf_op jit(solution)/shard_map/ppermute | solution.py:704
  34.1 3.8 %collective-permute-done.4 = f32[5,16,4,256]{3,2,1,0:T(4,128)S(1)} collective-permute-done((f32[5,16,4,256]{3,2,1,0:T(4,128)S(1)}, f32[5,16,4,256]{3,2,1,0:T(4,128)S(1)}, u32[]{:S(2)}, u32[]{:S(2)}) %collective-permute-start.4) | collective-permute-done | bytes 327712 | tf_op jit(solution)/shard_map/ppermute | solution.py:704
  37.9 0.2 pad_maximum_fusion.ext
  38.1 0.0 copy-done.4
  38.1 4.0 %shard_map.59 = (f32[80,128]{1,0:T(8,128)S(1)}, f32[3,8,8,256]{3,2,1,0:T(8,128)S(1)}, f32[3,8,8,128]{3,2,1,0:T(8,128)S(1)}, f32[3,17,16,256]{3,2,1,0:T(8,128)S(1)}) custom-call(f32[2,16]{1,0:T(2,128)S(1)} %copy-done.4, f32[5,16,16,256]{3,2,1,0:T(8,128)S(1)} %pad_maximum_fusion.ext), custom_call_target="tpu_custom_call" | custom-call | tf_op jit(solution)/shard_map/pallas_call | solution.py:663
  42.1 1.2 broadcast_in_dim.29
  43.3 11.0 %all-to-all-start = ((f32[32,80,128]{2,1,0:T(8,128)}), f32[32,80,128]{2,1,0:T(8,128)S(1)}, u32[]{:S(2)}, u32[]{:S(2)}) async-start(f32[32,80,128]{2,1,0:T(8,128)} %broadcast_in_dim.29), calls=%async_computation | async-start | bytes 2621440 | tf_op jit(solution)/shard_map/all_to_all | solution.py:726
  54.3 3.1 %collective-permute-start.6 = (f32[3,3,8,256]{3,2,1,0:T(8,128)S(1)}, f32[3,3,8,256]{3,2,1,0:T(8,128)S(1)}, u32[]{:S(2)}, u32[]{:S(2)}) collective-permute-start(f32[3,3,8,256]{3,2,1,0:T(8,128)S(1)} %get-tuple-element.31), channel_id=1, source_target_pairs={{0,64},{64,128},{128,192},{192,256},{256,320},{320,384},{384,448},... | collective-permute-start | bytes 221192 | tf_op jit(solution)/shard_map/ppermute | solution.py:704
  57.5 1.3 collective-permute-start.7
  58.8 23.7 %collective-permute-done.6 = f32[3,3,8,256]{3,2,1,0:T(8,128)S(1)} collective-permute-done((f32[3,3,8,256]{3,2,1,0:T(8,128)S(1)}, f32[3,3,8,256]{3,2,1,0:T(8,128)S(1)}, u32[]{:S(2)}, u32[]{:S(2)}) %collective-permute-start.6) | collective-permute-done | bytes 73760 | tf_op jit(solution)/shard_map/ppermute | solution.py:704
  82.5 2.7 %collective-permute-done.7 = f32[3,3,8,256]{3,2,1,0:T(8,128)S(1)} collective-permute-done((f32[3,3,8,256]{3,2,1,0:T(8,128)S(1)}, f32[3,3,8,256]{3,2,1,0:T(8,128)S(1)}, u32[]{:S(2)}, u32[]{:S(2)}) %collective-permute-start.7) | collective-permute-done | bytes 73760 | tf_op jit(solution)/shard_map/ppermute | solution.py:704
  85.1 0.0 copy-start.5
  85.1 0.7 copy-done.5
  85.9 1.1 all-to-all-done.got
  87.0 8.5 %shard_map.60 = (f32[2,16,128]{2,1,0:T(8,128)S(1)}, f32[3,34,16,128]{3,2,1,0:T(8,128)S(1)}, f32[3,34,16,128]{3,2,1,0:T(8,128)S(1)}, f32[3,34,16,128]{3,2,1,0:T(8...) custom-call(f32[32,80,128]{2,1,0:T(8,128)S(1)} %all-to-all-done.got), custom_call_target="tpu_custom_call" | custom-call | tf_op jit(solution)/shard_map/pallas_call | solution.py:675
  95.5 0.0 copy-start
  95.5 0.9 copy-done
  96.4 0.0 copy-start.2
  96.4 0.9 copy-done.2
  97.4 0.0 copy-start.6
  97.4 0.7 broadcast_in_dim.30
  98.1 8.6 %all-to-all-start.1 = ((f32[16,2,16,128]{3,2,1,0:T(8,128)}), f32[16,2,16,128]{3,2,1,0:T(8,128)S(1)}, u32[]{:S(2)}, u32[]{:S(2)}) async-start(f32[16,2,16,128]{3,2,1,0:T(8,128)} %broadcast_in_dim.30), calls=%async_computation.1 | async-start | bytes 524288 | tf_op jit(solution)/shard_map/all_to_all | solution.py:726
  106.7 1.1 fusion.1
  107.8 3.6 %collective-permute-start.9 = (f32[3,14,4,256]{3,2,1,0:T(4,128)S(1)}, f32[3,14,4,256]{3,2,1,0:T(4,128)S(1)}, u32[]{:S(2)}, u32[]{:S(2)}) collective-permute-start(f32[3,14,4,256]{3,2,1,0:T(4,128)S(1)} %get-tuple-element.27), channel_id=1, source_target_pairs={{0,16},{16,32},{32,48},{1,17},{17,33},{33,49},{2,18},{18,34},{34,5... | collective-permute-start | bytes 516104 | tf_op jit(solution)/shard_map/ppermute | solution.py:704
  111.4 1.5 collective-permute-start.8
  112.9 0.1 pad_add_fusion.place
  112.9 2.1 %collective-permute-done.9 = f32[3,14,4,256]{3,2,1,0:T(4,128)S(1)} collective-permute-done((f32[3,14,4,256]{3,2,1,0:T(4,128)S(1)}, f32[3,14,4,256]{3,2,1,0:T(4,128)S(1)}, u32[]{:S(2)}, u32[]{:S(2)}) %collective-permute-start.9) | collective-permute-done | bytes 172064 | tf_op jit(solution)/shard_map/ppermute | solution.py:704
  115.1 3.9 %collective-permute-done.8 = f32[3,14,4,256]{3,2,1,0:T(4,128)} collective-permute-done((f32[3,14,4,256]{3,2,1,0:T(4,128)S(1)}, f32[3,14,4,256]{3,2,1,0:T(4,128)}, u32[]{:S(2)}, u32[]{:S(2)}) %collective-permute-start.8) | collective-permute-done | bytes 172064 | tf_op jit(solution)/shard_map/ppermute | solution.py:704
  119.0 0.0 copy-done.6
  119.0 1.0 pad_maximum_fusion.1.r0
  120.0 0.0 all-to-all-done.1.got
  120.0 0.0 copy-start.1
  120.0 1.1 copy-done.1
  121.2 0.0 copy-start.3
  121.2 1.1 copy-done.3
  122.3 27.3 %shard_map.61 = (f32[3,8,8,128]{3,2,1,0:T(8,128)}, f32[3,8,8,128]{3,2,1,0:T(8,128)}) custom-call(s32[3]{0:T(128)S(1)} %pad_add_fusion.place, f32[16,2,16,128]{3,2,1,0:T(8,128)S(1)} %all-to-all-done.1.got, f32[3,34,16,128]{3,2,1,0:T(8,128)S(1)} %get-tuple-element.15.mod1, f32[3,34,16,128]{3,2,1,0:T(8,128)S(1)} %copy-done.1, f32[3,34,16,128]{3,2,1,0:T(8,128)S(1)} %copy-done.3, ...), custom_call_target="tpu_custom_call" | custom-call | tf_op jit(solution)/shard_map/pallas_call | solution.py:687
  (7 shorter events, 0.1 us)
Async XLA Ops:
  0.6 25.0 %copy-start.7 = (f32[3,8,8,128]{3,2,1,0:T(8,128)S(1)}, f32[3,8,8,128]{3,2,1,0:T(8,128)}, u32[]{:S(2)}) copy-start(f32[3,8,8,128]{3,2,1,0:T(8,128)} %param.4) | copy-start | bytes 294916
  2.4 10.7 %collective-permute-start = (f32[5,8,8,128]{3,2,1,0:T(8,128)S(1)}, f32[5,8,8,128]{3,2,1,0:T(8,128)S(1)}, u32[]{:S(2)}, u32[]{:S(2)}) collective-permute-start(f32[5,8,8,128]{3,2,1,0:T(8,128)S(1)} %pad_maximum_fusion.4), channel_id=1, source_target_pairs={{1,0},{2,1},{3,2},{4,3},{5,4},{6,5},{7,6},{8,7},{9,8},{10,9},{11,1... | collective-permute-start | bytes 491528 | tf_op jit(solution)/shard_map/ppermute | solution.py:704
  11.2 4.2 %collective-permute-start.1 = (f32[5,8,8,128]{3,2,1,0:T(8,128)S(1)}, f32[5,8,8,128]{3,2,1,0:T(8,128)S(1)}, u32[]{:S(2)}, u32[]{:S(2)}) collective-permute-start(f32[5,8,8,128]{3,2,1,0:T(8,128)S(1)} %pad_maximum_fusion.4), channel_id=1, source_target_pairs={{0,1},{1,2},{2,3},{3,4},{4,5},{5,6},{6,7},{7,8},{8,9},{9,10},{10,1... | collective-permute-start | bytes 491528 | tf_op jit(solution)/shard_map/ppermute | solution.py:704
  16.3 7.6 %collective-permute-start.3 = (f32[5,4,8,256]{3,2,1,0:T(8,128)S(1)}, f32[5,4,8,256]{3,2,1,0:T(8,128)S(1)}, u32[]{:S(2)}, u32[]{:S(2)}) collective-permute-start(f32[5,4,8,256]{3,2,1,0:T(8,128)S(1)} %get-tuple-element.29), channel_id=1, source_target_pairs={{64,0},{128,64},{192,128},{256,192},{320,256},{384,320},{448,384},... | collective-permute-start | bytes 491528 | tf_op jit(solution)/shard_map/ppermute | solution.py:704
  17.6 8.0 %collective-permute-start.2 = (f32[5,4,8,256]{3,2,1,0:T(8,128)S(1)}, f32[5,4,8,256]{3,2,1,0:T(8,128)S(1)}, u32[]{:S(2)}, u32[]{:S(2)}) collective-permute-start(f32[5,4,8,256]{3,2,1,0:T(8,128)S(1)} %get-tuple-element.28), channel_id=1, source_target_pairs={{0,64},{64,128},{128,192},{192,256},{256,320},{320,384},{384,448},... | collective-permute-start | bytes 491528 | tf_op jit(solution)/shard_map/ppermute | solution.py:704
  25.8 8.3 %collective-permute-start.5 = (f32[5,16,4,256]{3,2,1,0:T(4,128)S(1)}, f32[5,16,4,256]{3,2,1,0:T(4,128)S(1)}, u32[]{:S(2)}, u32[]{:S(2)}) collective-permute-start(f32[5,16,4,256]{3,2,1,0:T(4,128)S(1)} %get-tuple-element.25), channel_id=1, source_target_pairs={{0,16},{16,32},{32,48},{1,17},{17,33},{33,49},{2,18},{18,34},{34,5... | collective-permute-start | bytes 983048 | tf_op jit(solution)/shard_map/ppermute | solution.py:704
  27.1 11.0 %copy-start.4 = (f32[2,16]{1,0:T(2,128)S(1)}, f32[2,16]{1,0:T(2,128)}, u32[]{:S(2)}) copy-start(f32[2,16]{1,0:T(2,128)} %moduli.1) | copy-start | bytes 388
  27.1 10.8 %collective-permute-start.4 = (f32[5,16,4,256]{3,2,1,0:T(4,128)S(1)}, f32[5,16,4,256]{3,2,1,0:T(4,128)S(1)}, u32[]{:S(2)}, u32[]{:S(2)}) collective-permute-start(f32[5,16,4,256]{3,2,1,0:T(4,128)S(1)} %get-tuple-element.24), channel_id=1, source_target_pairs={{16,0},{32,16},{48,32},{17,1},{33,17},{49,33},{18,2},{34,18},{50,3... | collective-permute-start | bytes 983048 | tf_op jit(solution)/shard_map/ppermute | solution.py:704
  43.3 43.7 %all-to-all-start = ((f32[32,80,128]{2,1,0:T(8,128)}), f32[32,80,128]{2,1,0:T(8,128)S(1)}, u32[]{:S(2)}, u32[]{:S(2)}) async-start(f32[32,80,128]{2,1,0:T(8,128)} %broadcast_in_dim.29), calls=%async_computation | async-start | bytes 2621440 | tf_op jit(solution)/shard_map/all_to_all | solution.py:726
  54.3 28.1 %collective-permute-start.6 = (f32[3,3,8,256]{3,2,1,0:T(8,128)S(1)}, f32[3,3,8,256]{3,2,1,0:T(8,128)S(1)}, u32[]{:S(2)}, u32[]{:S(2)}) collective-permute-start(f32[3,3,8,256]{3,2,1,0:T(8,128)S(1)} %get-tuple-element.31), channel_id=1, source_target_pairs={{0,64},{64,128},{128,192},{192,256},{256,320},{320,384},{384,448},... | collective-permute-start | bytes 221192 | tf_op jit(solution)/shard_map/ppermute | solution.py:704
  57.5 27.6 %collective-permute-start.7 = (f32[3,3,8,256]{3,2,1,0:T(8,128)S(1)}, f32[3,3,8,256]{3,2,1,0:T(8,128)S(1)}, u32[]{:S(2)}, u32[]{:S(2)}) collective-permute-start(f32[3,3,8,256]{3,2,1,0:T(8,128)S(1)} %get-tuple-element.30), channel_id=1, source_target_pairs={{64,0},{128,64},{192,128},{256,192},{320,256},{384,320},{448,384},... | collective-permute-start | bytes 221192 | tf_op jit(solution)/shard_map/ppermute | solution.py:704
  85.1 0.7 copy-start.5
  95.5 0.9 copy-start
  96.4 0.9 copy-start.2
  97.4 21.6 %copy-start.6 = (f32[3,14,8,256]{3,2,1,0:T(8,128)S(1)}, f32[3,14,8,256]{3,2,1,0:T(8,128)}, u32[]{:S(2)}) copy-start(f32[3,14,8,256]{3,2,1,0:T(8,128)} %copy-done.5) | copy-start | bytes 1032196
  98.1 21.9 %all-to-all-start.1 = ((f32[16,2,16,128]{3,2,1,0:T(8,128)}), f32[16,2,16,128]{3,2,1,0:T(8,128)S(1)}, u32[]{:S(2)}, u32[]{:S(2)}) async-start(f32[16,2,16,128]{3,2,1,0:T(8,128)} %broadcast_in_dim.30), calls=%async_computation.1 | async-start | bytes 524288 | tf_op jit(solution)/shard_map/all_to_all | solution.py:726
  107.8 7.3 %collective-permute-start.9 = (f32[3,14,4,256]{3,2,1,0:T(4,128)S(1)}, f32[3,14,4,256]{3,2,1,0:T(4,128)S(1)}, u32[]{:S(2)}, u32[]{:S(2)}) collective-permute-start(f32[3,14,4,256]{3,2,1,0:T(4,128)S(1)} %get-tuple-element.27), channel_id=1, source_target_pairs={{0,16},{16,32},{32,48},{1,17},{17,33},{33,49},{2,18},{18,34},{34,5... | collective-permute-start | bytes 516104 | tf_op jit(solution)/shard_map/ppermute | solution.py:704
  111.4 7.6 %collective-permute-start.8 = (f32[3,14,4,256]{3,2,1,0:T(4,128)S(1)}, f32[3,14,4,256]{3,2,1,0:T(4,128)}, u32[]{:S(2)}, u32[]{:S(2)}) collective-permute-start(f32[3,14,4,256]{3,2,1,0:T(4,128)S(1)} %get-tuple-element.26), channel_id=1, source_target_pairs={{16,0},{32,16},{48,32},{17,1},{33,17},{49,33},{18,2},{34,18},{50,3... | collective-permute-start | bytes 516104 | tf_op jit(solution)/shard_map/ppermute | solution.py:704
  120.0 1.2 copy-start.1
  121.2 1.1 copy-start.3
